TPU v7x, 512 devices: a whole 4x4x16 slice. The times are simulated.
512 devices in a mesh: facet: 16 (over z_hi, y), sub: 16 (over x, z_lo), vis: 2 (over core).
Axes of the slice: x: 4, y: 4, z: 16 (z_hi: 4, z_lo: 4; z = z_hi * 4 + z_lo), core: 2. Of those that a mesh axis runs over, the one named last changes fastest.
Arguments:
- facet_strips: float32 [16, 512, 4096], P('facet', 'vis'), may hold values from -6 to 6
- taper: float32 [16, 512, 512], P('sub', ('facet', 'vis')), may hold values from 0.3 to 3
- send_pick: int32 [16, 16, 2, 16], P('facet', 'sub', 'vis'), may hold values from 0 to 1
- bl_owner: int32 [16, 16, 2, 8], P('facet', 'sub', 'vis'), may hold values from 0 to 15
- phase_tiles: float32 [16, 16, 2, 8, 64, 128], P('facet', 'sub', 'vis'), may hold values from -6 to 6
- cell_offsets: int32 [16, 16, 2, 8, 2, 1024], P('facet', 'sub', 'vis'), may hold values from 0 to 63
Outputs:
- visibilities: float32 [16, 16, 2, 8, 2, 1024], P('facet', 'sub', 'vis')
All inputs are finite; a program needn't handle non-finite values.
Results may differ from a plain program's by a relative error of at most 0.0003.
Values sent between devices are 32-bit elements; how exact they have to be, the bound alone decides.
A program may use at most 64 MiB of HBM per device.

v0:
```python
import math

import jax
import jax.numpy as jnp
from jax import lax
from jax.sharding import PartitionSpec as P

sky_cells = 65536
HIGH = lax.Precision.HIGHEST


def sky_turns(left_ids, right_ids):
    left_ids = left_ids % sky_cells
    right_ids = right_ids % sky_cells
    low_byte = right_ids % 256
    high_byte = right_ids // 256
    return (left_ids * low_byte + left_ids * high_byte % 256 * 256) % sky_cells


def sky_table(left_ids, right_ids):
    angles = sky_turns(left_ids, right_ids).astype(jnp.float32) * (2.0 * math.pi / sky_cells)
    return (jnp.cos(angles), -jnp.sin(angles))


def unit_table(left_ids, right_ids, length, orient, factor):
    angles = (left_ids * right_ids % length).astype(jnp.float32) * (2.0 * math.pi / length)
    return (jnp.cos(angles) * factor, jnp.sin(angles) * (orient * factor))


def product(left_op, right_op):
    return jnp.dot(left_op, right_op, precision=HIGH, preferred_element_type=jnp.float32)


def right_mul(values, real_part, imag_part):
    halfway = values.shape[-1] // 2
    val_re = values[:, :halfway]
    val_im = values[:, halfway:]
    return jnp.concatenate(
        [
            product(val_re, real_part) - product(val_im, imag_part),
            product(val_re, imag_part) + product(val_im, real_part),
        ],
        axis=1,
    )


def left_mul(real_part, imag_part, values):
    halfway = values.shape[-1] // 2
    val_re = values[:, :halfway]
    val_im = values[:, halfway:]
    return jnp.concatenate(
        [
            product(real_part, val_re) - product(imag_part, val_im),
            product(real_part, val_im) + product(imag_part, val_re),
        ],
        axis=1,
    )


def strip_tables(facet_index, subgrid, row_start, row_count, col_count, grid_width):
    row_pos = facet_index * 4096 + row_start + jnp.arange(row_count, dtype=jnp.int32)
    col_pos = 5 * facet_index % 16 * 4096 + jnp.arange(col_count, dtype=jnp.int32)
    freqs = jnp.arange(grid_width, dtype=jnp.int32)
    row_freq = subgrid * 4099 + 257 * freqs
    col_freq = subgrid * 1031 + 33 * freqs
    left_re, left_im = sky_table(row_freq[:, None], row_pos[None, :])
    right_re, right_im = sky_table(col_pos[:, None], col_freq[None, :])
    return (left_re, left_im, right_re, right_im)


def degrid(picked, phase_tile, offsets):
    patch_size = picked.shape[-2]
    pick_re = picked[..., :patch_size]
    pick_im = picked[..., patch_size:]
    tile_re = phase_tile[..., :patch_size]
    tile_im = phase_tile[..., patch_size:]
    mixed_re = pick_re * tile_re - pick_im * tile_im
    mixed_im = pick_re * tile_im + pick_im * tile_re
    cells = jnp.arange(patch_size, dtype=jnp.int32)
    u_re, u_im = unit_table(cells[:, None], offsets[..., 0:1, :], patch_size, -1.0, 1.0)
    w_re, w_im = unit_table(cells[:, None], offsets[..., 1:2, :], patch_size, -1.0, 1.0)

    def contract(left_op, right_op):
        return jnp.einsum(
            "...ij,...ik->...jk",
            left_op,
            right_op,
            precision=HIGH,
            preferred_element_type=jnp.float32,
        )

    along_re = contract(mixed_re, u_re) - contract(mixed_im, u_im)
    along_im = contract(mixed_im, u_re) + contract(mixed_re, u_im)
    vis_re = jnp.sum(along_re * w_re - along_im * w_im, axis=-2) / patch_size
    vis_im = jnp.sum(along_re * w_im + along_im * w_re, axis=-2) / patch_size
    return jnp.stack([vis_re, vis_im], axis=-2)


def local(facet_strips, taper, send_pick, bl_owner, phase_tiles, cell_offsets):
    facet_index = lax.axis_index("facet")
    subgrid = lax.axis_index("sub")
    core_index = lax.axis_index("vis")
    n_facet = lax.axis_size("facet")
    n_core = lax.axis_size("vis")
    n_subgrid = lax.axis_size("sub")
    groups = n_facet * n_core
    strip_data = facet_strips[0]
    strip_rows = strip_data.shape[0]
    strip_cols = strip_data.shape[1] // 2
    grid_width = taper.shape[2]
    scaling = 1.0 / math.sqrt(strip_rows * n_core * strip_cols * n_facet)
    left_re, left_im, right_re, right_im = strip_tables(
        facet_index, subgrid, core_index * strip_rows, strip_rows, strip_cols, grid_width
    )
    spread = right_mul(strip_data, right_re, right_im)
    summed = lax.psum_scatter(
        left_mul(left_re, left_im, spread) * scaling,
        ("facet", "vis"),
        scatter_dimension=0,
        tiled=True,
    )
    window = taper[0]
    tapered = summed * jnp.concatenate([window, window], axis=1)
    cell_index = jnp.arange(grid_width, dtype=jnp.int32)
    q_re, q_im = unit_table(
        cell_index[:, None], cell_index[None, :], grid_width, 1.0, 1.0 / math.sqrt(grid_width)
    )
    mixed = right_mul(tapered, q_re, q_im)
    patch_size = phase_tiles.shape[4]
    per_side = grid_width // patch_size
    per_device = per_side * per_side // groups
    block_cols = per_device * patch_size
    across = grid_width // block_cols
    position = facet_index * n_core + core_index
    row_block = position // across
    col_block = position % across
    row_ids = row_block * patch_size + jnp.arange(patch_size, dtype=jnp.int32)
    p_re, p_im = unit_table(
        row_ids[:, None], cell_index[None, :], grid_width, 1.0, 1.0 / math.sqrt(grid_width)
    )
    incoming = lax.all_gather(mixed, ("facet", "vis"), axis=0, tiled=True)
    columns = jnp.concatenate(
        [
            lax.dynamic_slice_in_dim(incoming, col_block * block_cols, block_cols, 1),
            lax.dynamic_slice_in_dim(incoming, grid_width + col_block * block_cols, block_cols, 1),
        ],
        axis=1,
    )
    grid_block = left_mul(p_re, p_im, columns)
    patch_re = (
        grid_block[:, :block_cols].reshape(patch_size, per_device, patch_size).transpose(1, 0, 2)
    )
    patch_im = (
        grid_block[:, block_cols:].reshape(patch_size, per_device, patch_size).transpose(1, 0, 2)
    )
    own_patches = jnp.concatenate([patch_re, patch_im], axis=2)
    pick_row = send_pick[0, 0, 0]
    gathered, all_picks = (
        lax.all_gather(own_patches[None], "sub", axis=0, tiled=True),
        lax.all_gather(pick_row[None].astype(jnp.float32), "sub", axis=0, tiled=True),
    )
    my_picks = lax.dynamic_slice_in_dim(all_picks, subgrid, 1, 1)
    select = (my_picks == jnp.arange(per_device, dtype=jnp.float32)[None, :]).astype(jnp.float32)
    received = jnp.einsum(
        "oj,ojx->ox",
        select,
        gathered.reshape(n_subgrid, per_device, -1),
        precision=HIGH,
        preferred_element_type=jnp.float32,
    )
    received = received.reshape(n_subgrid, patch_size, 2 * patch_size)
    owners = bl_owner[0, 0, 0]
    owner_hot = (owners[:, None] == jnp.arange(n_subgrid, dtype=jnp.int32)[None, :]).astype(
        jnp.float32
    )
    picked = product(owner_hot, received.reshape(n_subgrid, -1)).reshape(
        -1, patch_size, 2 * patch_size
    )
    result = degrid(picked, phase_tiles[0, 0, 0], cell_offsets[0, 0, 0])
    return result[None, None, None]


def solution(mesh):
    placed = (
        P("facet", "vis", None),
        P("sub", ("facet", "vis"), None),
        P("facet", "sub", "vis", None),
        P("facet", "sub", "vis", None),
        P("facet", "sub", "vis", None, None, None),
        P("facet", "sub", "vis", None, None, None),
    )
    return jax.shard_map(
        local,
        mesh=mesh,
        in_specs=placed,
        out_specs=P("facet", "sub", "vis", None, None, None),
        check_vma=False,
    )
```

profile of v0, /device:TPU:8, one launch (start us, length us, event | category | flops | bytes accessed | tf_op | source)
XLA Modules:
  0.0 515.7 jit_solution(7721810106865060915)
XLA Ops:
  6.6 26.6 %fusion.6 = f32[512,256]{1,0:T(8,128)S(1)} fusion(s32[512]{0:T(512)S(1)} %get-tuple-element.13, s32[512]{0:T(512)S(1)} %get-tuple-element.14, s32[2048]{0:T(1024)S(1)} %add_select_fusion.8, f32[256,4096]{1,0:T(8,128)} %bitcast.42), kind=kOutput, calls=%fused_computation.15 | convolution fusion | flops 3251634176 | bytes 2633728 | tf_op jit(solution)/shard_map/dot_general | solution.py:31
  33.2 25.4 %fusion.7 = f32[512,256]{1,0:T(8,128)S(1)} fusion(s32[512]{0:T(512)S(1)} %get-tuple-element.13, s32[512]{0:T(512)S(1)} %get-tuple-element.14, s32[2048]{0:T(1024)S(1)} %add_select_fusion.8, f32[256,4096]{1,0:T(8,128)S(1)} %bitcast.44), kind=kOutput, calls=%fused_computation.16 | convolution fusion | flops 3251634176 | bytes 2633728 | tf_op jit(solution)/shard_map/dot_general | solution.py:31
  58.6 25.2 %fusion.40 = f32[512,256]{1,0:T(8,128)S(1)} fusion(f32[512,256]{1,0:T(8,128)S(1)} %fusion.6, f32[256,4096]{1,0:T(8,128)S(1)} %bitcast.45, s32[512]{0:T(512)S(1)} %get-tuple-element.13, s32[512]{0:T(512)S(1)} %get-tuple-element.14, s32[2048]{0:T(1024)S(1)} %add_select_fusion.8), kind=kOutput, calls=%fused_computation.57 | convolution fusion | flops 3250716672 | bytes 3158016 | tf_op jit(solution)/shard_map/dot_general | solution.py:31
  83.8 37.1 %fusion.35 = f32[512,256]{1,0:T(8,128)S(1)} fusion(f32[512,256]{1,0:T(8,128)S(1)} %fusion.7, f32[256,4096]{1,0:T(8,128)} %bitcast.43, s32[512]{0:T(512)S(1)} %get-tuple-element.13, s32[512]{0:T(512)S(1)} %get-tuple-element.14, s32[2048]{0:T(1024)S(1)} %add_select_fusion.8), kind=kOutput, calls=%fused_computation.56 | convolution fusion | flops 3250716672 | bytes 3158016 | tf_op jit(solution)/shard_map/dot_general | solution.py:31
  120.9 3.3 fusion.82
  124.2 3.3 fusion.84
  127.5 3.3 convolution_add_fusion
  130.8 3.7 convolution_subtract_fusion
  134.8 1.9 copy.41
  136.7 0.7 copy-done.2
  137.6 124.4 %reduce-scatter.4.cloned.1.call-done = f32[16,1024]{1,0:T(8,128)} async-done(((f32[512,1024]{1,0:T(8,128)}), f32[16,1024]{1,0:T(8,128)}) %reduce-scatter.4.cloned.1.call-update) | async-done | bytes 65552
  261.9 1.0 copy.42
  263.1 4.7 fusion.62
  267.8 4.7 fusion.61
  272.5 4.7 convolution_add_fusion.2
  277.2 4.7 convolution_subtract_fusion.2
  282.0 0.6 pad_maximum_fusion.1
  282.9 73.8 %all-gather.5.cloned.1.call-done = f32[512,1024]{1,0:T(8,128)} async-done(((f32[16,1024]{1,0:T(8,128)}), f32[512,1024]{1,0:T(8,128)}) %all-gather.5.cloned.1.call-update) | async-done | bytes 2097168 | tf_op jit(solution)/shard_map/all_gather | solution.py:141
  356.7 1.8 fusion.90
  358.5 1.8 convolution_add_fusion.1
  360.5 1.8 fusion.94
  362.3 1.8 convolution_subtract_fusion.1
  364.2 0.7 pad_maximum_fusion.2
  365.0 39.3 %all-gather = f32[16,1,1,16]{3,2,1,0:T(1,128)S(1)} all-gather(f32[1,1,1,16]{3,2,1,0:T(1,128)S(1)} %convert_element_type.40), channel_id=2, replica_groups=mesh['facet'=16,'sub'=16,'vis'=2] {'sub'}, dimensions={0}, use_global_device_ids=true | all-gather | bytes 1088 | tf_op jit(solution)/shard_map/all_gather | solution.py:160
  404.8 42.0 %all-gather.7.cloned.1.call-done = f32[32,64,128]{2,1,0:T(8,128)} async-done(((f32[2,64,128]{2,1,0:T(8,128)}), f32[32,64,128]{2,1,0:T(8,128)}) %all-gather.7.cloned.1.call-update) | async-done | bytes 1048592 | tf_op jit(solution)/shard_map/all_gather | solution.py:159
  446.8 1.8 reshape.240
  448.7 2.1 fusion.110
  451.8 12.2 %fusion.56 = f32[8,64,1024]{2,1,0:T(8,128)S(1)} fusion(f32[8,64,64]{2,1,0:T(8,128)S(1)} %get-tuple-element.7, s32[8,1024]{1,0:T(8,128)S(1)} %get-tuple-element.18), kind=kOutput, calls=%fused_computation.71 | convolution fusion | flops 409993216 | bytes 2260992 | tf_op jit(solution)/shard_map/...ij,...ik->...jk/dot_general | solution.py:84
  464.0 12.2 %fusion.54 = f32[8,64,1024]{2,1,0:T(8,128)S(1)} fusion(f32[8,64,64]{2,1,0:T(8,128)S(1)} %get-tuple-element.8, s32[8,1024]{1,0:T(8,128)S(1)} %get-tuple-element.18), kind=kOutput, calls=%fused_computation.70 | convolution fusion | flops 409993216 | bytes 2260992 | tf_op jit(solution)/shard_map/...ij,...ik->...jk/dot_general | solution.py:84
  476.3 12.3 %fusion.33 = f32[8,64,1024]{2,1,0:T(8,128)S(1)} fusion(f32[8,64,1024]{2,1,0:T(8,128)S(1)} %fusion.56, f32[8,64,64]{2,1,0:T(8,128)S(1)} %get-tuple-element.8, s32[8,1024]{1,0:T(8,128)S(1)} %get-tuple-element.18), kind=kOutput, calls=%fused_computation.49 | convolution fusion | flops 411041792 | bytes 4358144 | tf_op jit(solution)/shard_map/...ij,...ik->...jk/dot_general | solution.py:84
  488.5 19.7 %subtract_reduce_fusion = (f32[8,1024]{1,0:T(8,128)S(1)}, f32[8,1024]{1,0:T(8,128)S(1)}) fusion(f32[8,64,1024]{2,1,0:T(8,128)S(1)} %fusion.33, s32[8,1024]{1,0:T(8,128)S(1)} %get-tuple-element.17, f32[8,64,1024]{2,1,0:T(8,128)S(1)} %fusion.54, f32[8,64,64]{2,1,0:T(8,128)S(1)} %get-tuple-element.7, s32[8,1024]{1,0:T(8,128)S(1)} %get-tuple-element.18), kind=kOutput, calls=%fused_computation.31 | convolution fusion | flops 423084032 | bytes 4456448 | tf_op jit(solution)/shard_map/...ij,...ik->...jk/dot_general | solution.py:84
  508.3 0.7 maximum_bitcast_fusion
  (42 shorter events, 2.6 us)
Async XLA Ops:
  6.5 255.4 %reduce-scatter.4.cloned.1.call-start = ((), (), s32[]{:S(2)}) async-start(), calls=%async_computation.3 | async-start | bytes 2162688
  6.6 26.6 %copy-start.4 = (f32[1,256,4096]{2,1,0:T(8,128)S(1)}, f32[1,256,4096]{2,1,0:T(8,128)}, u32[]{:S(2)}) copy-start(f32[1,256,4096]{2,1,0:T(8,128)} %param.6) | copy-start | bytes 12582916
  136.6 0.8 copy-start.2
  136.6 220.1 %all-gather.5.cloned.1.call-start = ((), (), s32[]{:S(2)}) async-start(), calls=%async_computation.1 | async-start | bytes 2162688 | tf_op jit(solution)/shard_map/all_gather | solution.py:141
  281.9 83.0 %copy-start.5 = (s32[1,1,1,16]{3,2,1,0:T(1,128)S(1)}, s32[1,1,1,16]{3,2,1,0:T(1,128)}, u32[]{:S(2)}) copy-start(s32[1,1,1,16]{3,2,1,0:T(1,128)} %param.8) | copy-start | bytes 196
  281.9 122.7 %copy-start.1 = (s32[1,1,1,8,2,1024]{5,4,3,2,1,0:T(2,128)S(1)}, s32[1,1,1,8,2,1024]{5,4,3,2,1,0:T(2,128)}, u32[]{:S(2)}) copy-start(s32[1,1,1,8,2,1024]{5,4,3,2,1,0:T(2,128)} %param.11) | copy-start | bytes 196612
  282.6 164.2 %all-gather.7.cloned.1.call-start = ((), (), s32[]{:S(2)}) async-start(), calls=%async_computation.2 | async-start | bytes 1114112 | tf_op jit(solution)/shard_map/all_gather | solution.py:159
  404.7 46.0 %copy-start.3 = (s32[1,1,1,8]{3,2,1,0:T(1,128)S(1)}, s32[1,1,1,8]{3,2,1,0:T(1,128)}, u32[]{:S(2)}) copy-start(s32[1,1,1,8]{3,2,1,0:T(1,128)} %param.9) | copy-start | bytes 100
  448.6 2.9 copy-start
Sparse Core Ops, SparseCore 0:
  136.8 125.1 reduce-scatter.3
  282.7 73.9 all-gather.4
  365.1 81.6 all-gather.6
where the time goes:
time: 518 us; the launch traced here: 516 us
  waiting for transfers between devices  240 us (46%)
  matrix products  213 us (41%)
  blocking collectives  39.3 us (8%)
  between operations  13.7 us (3%)
  local copies, waits for them, and re-layouts  6.38 us (1%)
    dot_general x17, matrix products, product(): jnp.dot(left_op, right_op, precision=HIGH, preferred_element_type=jnp.flo...  155 us
    unnamed x4, waiting for transfers between devices  124 us
    all_gather x1, waiting for transfers between devices, local(): incoming = lax.all_gather(mixed, ('facet', 'vis'), axis=0, tiled=True)  73.8 us
    dot_general x4, matrix products, contract(): jnp.einsum('...ij,...ik->...jk', left_op, right_op, precision=HIGH, prefe...  56.4 us
    all_gather x1, waiting for transfers between devices, local(): lax.all_gather(own_patches[None], 'sub', axis=0, tiled=True)  42 us
    all_gather x1, blocking collectives, local(): lax.all_gather(pick_row[None].astype(jnp.float32), 'sub', axis=0, tiled=T...  39.3 us
  transfers between devices with their start and end apart: 3, of which 3 were waited for; matrix products, arithmetic and copies ran while one was open for 0% of the time, Pallas kernels for 0%

commit v1 on v0

v1 whole, which is shorter than its diff:
```python
import functools
import math

import jax
import jax.numpy as jnp
import ml_dtypes
import numpy as np
from jax import lax
from jax.experimental import pallas as pl
from jax.experimental.pallas import tpu as pltpu
from jax.sharding import PartitionSpec as P

MESH = pl.DeviceIdType.MESH
F32 = jnp.float32
BF16 = jnp.bfloat16
VM = pl.BlockSpec(memory_space=pltpu.VMEM)
SCALE = 1.0 / math.sqrt(512 * 2048 * 16)


def halves(table):
    high = table.astype(np.float32).astype(ml_dtypes.bfloat16)
    low = (table - high.astype(np.float64)).astype(ml_dtypes.bfloat16)
    return high, low


@functools.lru_cache(None)
def column_table():
    freq = np.arange(512)[:, None]
    cols = np.arange(2048)[None, :]
    angle = (33 * freq * cols % 65536) * (2.0 * np.pi / 65536)
    both = np.stack([np.cos(angle).reshape(32, 16, 2048), -np.sin(angle).reshape(32, 16, 2048)], 1)
    return halves(both.reshape(1024, 2048))


@functools.lru_cache(None)
def row_table():
    rows = np.arange(256)[:, None]
    freq = np.arange(512)[None, :]
    angle = (257 * freq * rows % 65536) * (2.0 * np.pi / 65536)
    return halves(np.concatenate([np.cos(angle), -np.sin(angle)], 1))


@functools.lru_cache(None)
def grid_table():
    left = np.arange(512)[:, None]
    right = np.arange(512)[None, :]
    angle = (left * right % 512) * (2.0 * np.pi / 512)
    scale = 1.0 / math.sqrt(512)
    both = np.stack(
        [np.cos(angle).reshape(512, 8, 64) * scale, np.sin(angle).reshape(512, 8, 64) * scale], 2
    )
    return halves(both.reshape(512, 1024))


@functools.lru_cache(None)
def cell_tables():
    left = np.arange(64)[:, None]
    right = np.arange(64)[None, :]
    angle = (left * right % 64) * (2.0 * np.pi / 64)
    cos, sin = np.cos(angle) / 8.0, -np.sin(angle) / 8.0
    square = np.concatenate(
        [np.concatenate([cos, sin], 1), np.concatenate([-sin, cos], 1)], 0
    )
    flat = np.concatenate([cos, sin], 1)
    return halves(square) + halves(flat)


def split(value):
    high = value.astype(BF16)
    return high, (value - high.astype(F32)).astype(BF16)


def dot(left, right):
    return jnp.dot(left, right, preferred_element_type=F32)


def dot_t(left, right):
    return lax.dot_general(left, right, (((1,), (1,)), ((), ())), preferred_element_type=F32)


def dot3(left, right_high, right_low):
    high, low = split(left)
    return dot(high, right_high) + dot(low, right_high) + dot(high, right_low)


def turned(turns, modulus):
    angles = (turns & (modulus - 1)).astype(F32) * (2.0 * math.pi / modulus)
    return jnp.cos(angles), -jnp.sin(angles)


def iota(shape, dim):
    return lax.broadcasted_iota(jnp.int32, shape, dim)


def strip_kernel(place, re_ref, im_ref, th_ref, tl_ref, lh_ref, ll_ref, out_ref, acc):
    step = pl.program_id(0)
    facet, sub, core = place[0], place[1], place[2]
    width = re_ref.shape[1]
    cols = step * width + iota((8, width), 1)
    c_re, c_im = turned(sub * 1031 * cols, 65536)
    c_re, c_im = c_re[0:1], c_im[0:1]
    s_re, s_im = re_ref[...], im_ref[...]
    moved = jnp.concatenate([s_re * c_re - s_im * c_im, s_re * c_im + s_im * c_re], 0)
    high, low = split(moved)
    t_high = th_ref[...]
    more = dot_t(t_high, high) + dot_t(t_high, low) + dot_t(tl_ref[...], high)

    @pl.when(step == 0)
    def _():
        acc[...] = more

    @pl.when(step > 0)
    def _():
        acc[...] += more

    @pl.when(step == pl.num_programs(0) - 1)
    def _():
        rows = core * 256 + iota((8, 256), 1)
        r_re, r_im = turned(sub * 4099 * rows, 65536)
        r_re, r_im = r_re[0:1], r_im[0:1]
        freq = iota((16, 512), 1)
        other = iota((16, 512), 0)
        turn = facet * ((freq + 5 * other + 6 * sub) & 15) * 16 + freq * core
        w_re, w_im = turned(turn, 256)
        w_re, w_im = w_re * SCALE, w_im * SCALE

        def chunk(index, carry):
            where = pl.ds(pl.multiple_of(index * 256, 256), 256)
            part = acc[where, :].reshape(8, 2, 16, 512)
            q_re, q_im = part[:, 0], part[:, 1]
            a_re = q_re[..., :256] - q_im[..., 256:]
            a_im = q_re[..., 256:] + q_im[..., :256]
            turned_re = a_re * r_re - a_im * r_im
            turned_im = a_re * r_im + a_im * r_re
            both = jnp.stack([turned_re, turned_im], 1).reshape(256, 256)
            prod = dot3(both, lh_ref[...], ll_ref[...]).reshape(8, 2, 16, 1024)
            p_re, p_im = prod[:, 0], prod[:, 1]
            o_re = p_re[..., :512] - p_im[..., 512:]
            o_im = p_re[..., 512:] + p_im[..., :512]
            out_re = o_re * w_re - o_im * w_im
            out_im = o_re * w_im + o_im * w_re
            out_ref[where, :] = jnp.stack([out_re, out_im], 1).reshape(256, 512)
            return carry

        lax.fori_loop(0, 4, chunk, 0)


def strip_part(place, strip):
    steps = 4
    width = 2048 // steps
    t_high, t_low = (jnp.asarray(x) for x in column_table())
    l_high, l_low = (jnp.asarray(x) for x in row_table())
    whole = pl.BlockSpec((256, 1024), lambda i, p: (0, 0))
    return pl.pallas_call(
        strip_kernel,
        out_shape=jax.ShapeDtypeStruct((1024, 512), F32),
        grid_spec=pltpu.PrefetchScalarGridSpec(
            num_scalar_prefetch=1,
            grid=(steps,),
            in_specs=[
                pl.BlockSpec((256, width), lambda i, p: (0, i)),
                pl.BlockSpec((256, width), lambda i, p: (0, i + steps)),
                pl.BlockSpec((1024, width), lambda i, p: (0, i)),
                pl.BlockSpec((1024, width), lambda i, p: (0, i)),
                whole,
                whole,
            ],
            out_specs=pl.BlockSpec((1024, 512), lambda i, p: (0, 0)),
            scratch_shapes=[pltpu.VMEM((1024, 512), F32)],
        ),
        compiler_params=pltpu.CompilerParams(vmem_limit_bytes=56 << 20),
    )(place, strip, strip, t_high, t_low, l_high, l_low)


def here():
    facet, sub, core = lax.axis_index("facet"), lax.axis_index("sub"), lax.axis_index("vis")
    return facet // 4, facet % 4, sub // 4, sub % 4, core


def sum_kernel(
    part, tap, sum_out, tap_out, got_core, half, got_y, to_z, got_z,
    core_send, core_recv, y_send, y_recv, z_send, z_recv, t_send, t_recv,
):
    z, y, _, _, c = here()
    me = (z * 4 + y) * 2 + c
    barrier = pltpu.get_barrier_semaphore()

    def greet(step, carry):
        peer = (me + step) % 32
        pl.semaphore_signal(
            barrier, inc=1, device_id={"facet": peer // 2, "vis": peer % 2}, device_id_type=MESH
        )
        return carry

    lax.fori_loop(1, 32, greet, 0)
    pl.semaphore_wait(barrier, 31)

    def core_copy(at):
        return pltpu.make_async_remote_copy(
            src_ref=part.at[1 - c, :, at], dst_ref=got_core.at[:, at],
            send_sem=core_send.at[at], recv_sem=core_recv.at[at],
            device_id={"vis": 1 - c}, device_id_type=MESH,
        )

    def y_copy(dy, at):
        to = (y + dy) % 4
        return pltpu.make_async_remote_copy(
            src_ref=half.at[to, at], dst_ref=got_y.at[dy - 1, at],
            send_sem=y_send.at[dy - 1, at], recv_sem=y_recv.at[dy - 1, at],
            device_id={"facet": z * 4 + to}, device_id_type=MESH,
        )

    def z_copy(dz):
        to = (z + dz) % 4
        return pltpu.make_async_remote_copy(
            src_ref=to_z.at[dz - 1], dst_ref=got_z.at[dz - 1],
            send_sem=z_send.at[dz - 1], recv_sem=z_recv.at[dz - 1],
            device_id={"facet": to * 4 + y}, device_id_type=MESH,
        )

    def tap_copy(step):
        peer = (me + step) % 32
        block = (peer % 2) * 16 + (peer // 2 % 4) * 4 + peer // 8
        return pltpu.make_async_remote_copy(
            src_ref=tap.at[block], dst_ref=tap_out.at[me],
            send_sem=t_send.at[step], recv_sem=t_recv.at[step],
            device_id={"facet": peer // 2, "vis": peer % 2}, device_id_type=MESH,
        )

    def tap_arrival(step):
        source = (me - step + 32) % 32
        return pltpu.make_async_remote_copy(
            src_ref=tap.at[0], dst_ref=tap_out.at[source],
            send_sem=t_send.at[step], recv_sem=t_recv.at[step],
            device_id={"facet": source // 2, "vis": source % 2}, device_id_type=MESH,
        )

    order = (2, 1, 3, 0)
    for dz in order:
        core_copy((z + dz) % 4).start()

    def tap_start(step, carry):
        tap_copy(step).start()
        return carry

    lax.fori_loop(1, 32, tap_start, 0)
    tap_out[me] = tap[c * 16 + y * 4 + z]
    for dz in order:
        at = (z + dz) % 4
        core_copy(at).wait()
        for dy in (2, 1, 3, 0):
            to = (y + dy) % 4
            half[to, at] = part[c, to, at] + got_core[to, at]
            if dy:
                y_copy(dy, at).start()
    for dz in order:
        at = (z + dz) % 4
        for dy in (1, 3, 2):
            y_copy(dy, at).wait()
        total = (half[y, at] + got_y[0, at]) + (got_y[1, at] + got_y[2, at])
        if dz:
            to_z[dz - 1] = total
            z_copy(dz).start()
        else:
            sum_out[...] = total

    def tap_wait(step, carry):
        tap_copy(step).wait_send()
        tap_arrival(step).wait_recv()
        return carry

    lax.fori_loop(1, 32, tap_wait, 0)
    for dz in (1, 3, 2):
        z_copy(dz).wait()
    sum_out[...] += got_z[0] + got_z[1] + got_z[2]


def sum_over_facets(part, tap):
    dma = pltpu.SemaphoreType.DMA
    return pl.pallas_call(
        sum_kernel,
        out_shape=(
            jax.ShapeDtypeStruct((32, 512), F32),
            jax.ShapeDtypeStruct((32, 2, 128), F32),
        ),
        in_specs=[VM, VM],
        out_specs=(VM, VM),
        scratch_shapes=[
            pltpu.VMEM((4, 4, 32, 512), F32),
            pltpu.VMEM((4, 4, 32, 512), F32),
            pltpu.VMEM((3, 4, 32, 512), F32),
            pltpu.VMEM((3, 32, 512), F32),
            pltpu.VMEM((3, 32, 512), F32),
            dma((4,)), dma((4,)), dma((3, 4)), dma((3, 4)), dma((3,)), dma((3,)),
            dma((32,)), dma((32,)),
        ],
        compiler_params=pltpu.CompilerParams(
            collective_id=0, has_side_effects=True, vmem_limit_bytes=40 << 20
        ),
    )(part, tap)


def swapped(top, bottom):
    sign = jnp.where(iota(top.shape, 1) < 64, -1.0, 1.0).astype(F32)
    return top + pltpu.roll(bottom, 64, 1) * sign


def grid_kernel(
    sums, window, ph, pw, out, ubuf, zbuf, ybuf, z_send, z_recv, y_send, y_recv
):
    z, y, _, _, c = here()
    barrier = pltpu.get_barrier_semaphore()
    for dz in (1, 2, 3):
        pl.semaphore_signal(
            barrier, inc=1, device_id={"facet": (z + dz) % 4 * 4 + y}, device_id_type=MESH
        )
    near = [(dy, dc) for dy in range(4) for dc in range(2) if dy or dc]
    for dy, dc in near:
        pl.semaphore_signal(
            barrier, inc=1,
            device_id={"facet": z * 4 + (y + dy) % 4, "vis": (c + dc) % 2}, device_id_type=MESH,
        )
    taper = window[...]
    tapered = sums[...] * jnp.concatenate([taper, taper], 0)
    prod = dot3(tapered, ph[...], pw[...])
    for block in range(8):
        where = slice(block * 128, block * 128 + 128)
        ubuf[block // 2, block % 2] = swapped(prod[:16, where], prod[16:, where])
    pl.semaphore_wait(barrier, 10)

    def z_copy(dz):
        to = (z + dz) % 4
        return pltpu.make_async_remote_copy(
            src_ref=ubuf.at[to], dst_ref=zbuf.at[z],
            send_sem=z_send.at[dz - 1], recv_sem=z_recv.at[dz - 1],
            device_id={"facet": to * 4 + y}, device_id_type=MESH,
        )

    def z_arrival(dz):
        source = (z - dz + 4) % 4
        return pltpu.make_async_remote_copy(
            src_ref=ubuf.at[source], dst_ref=zbuf.at[source],
            send_sem=z_send.at[dz - 1], recv_sem=z_recv.at[dz - 1],
            device_id={"facet": source * 4 + y}, device_id_type=MESH,
        )

    def y_copy(index):
        dy, dc = near[index]
        to = (y + dy) % 4
        return pltpu.make_async_remote_copy(
            src_ref=zbuf.at[:, to // 2], dst_ref=ybuf.at[c, y],
            send_sem=y_send.at[index], recv_sem=y_recv.at[index],
            device_id={"facet": z * 4 + to, "vis": (c + dc) % 2}, device_id_type=MESH,
        )

    def y_arrival(index):
        dy, dc = near[index]
        source = (y - dy + 4) % 4
        return pltpu.make_async_remote_copy(
            src_ref=zbuf.at[:, 0], dst_ref=ybuf.at[(c + dc) % 2, source],
            send_sem=y_send.at[index], recv_sem=y_recv.at[index],
            device_id={"facet": z * 4 + source, "vis": (c + dc) % 2}, device_id_type=MESH,
        )

    for dz in (2, 1, 3):
        z_copy(dz).start()
    zbuf[z] = ubuf[z]
    for dz in (1, 3, 2):
        z_arrival(dz).wait_recv()
    for index in range(7):
        y_copy(index).start()
    ybuf[c, y] = zbuf[:, y // 2]
    for dz in (1, 2, 3):
        z_copy(dz).wait_send()
    for index in range(7):
        y_copy(index).wait_send()
        y_arrival(index).wait_recv()
    cols = ybuf[...].reshape(512, 128).T
    where = pl.ds(pl.multiple_of(((y % 2) * 2 + c) * 256, 256), 256)
    prod = dot3(cols, ph[:, where], pw[:, where])
    for j in range(2):
        where = slice(j * 128, j * 128 + 128)
        out[j] = swapped(prod[:64, where], prod[64:, where])


def grid_patches(sums, window):
    dma = pltpu.SemaphoreType.DMA
    ph, pw = (jnp.asarray(x) for x in grid_table())
    return pl.pallas_call(
        grid_kernel,
        out_shape=jax.ShapeDtypeStruct((2, 64, 128), F32),
        in_specs=[VM] * 4,
        out_specs=VM,
        scratch_shapes=[
            pltpu.VMEM((4, 2, 16, 128), F32),
            pltpu.VMEM((4, 2, 16, 128), F32),
            pltpu.VMEM((2, 4, 4, 16, 128), F32),
            dma((3,)), dma((3,)), dma((7,)), dma((7,)),
        ],
        compiler_params=pltpu.CompilerParams(
            collective_id=1, has_side_effects=True, vmem_limit_bytes=40 << 20
        ),
    )(sums, window, ph, pw)


def patch_kernel(
    own, picks, out, zpatch, zpick, staged, z_send, z_recv, p_send, p_recv, x_send, x_recv
):
    _, _, x, z, _ = here()
    barrier = pltpu.get_barrier_semaphore()
    for step in (1, 2, 3):
        pl.semaphore_signal(
            barrier, inc=1, device_id={"sub": x * 4 + (z + step) % 4}, device_id_type=MESH
        )
        pl.semaphore_signal(
            barrier, inc=1, device_id={"sub": (x + step) % 4 * 4 + z}, device_id_type=MESH
        )
    pl.semaphore_wait(barrier, 6)

    def z_copies(dz):
        to = (z + dz) % 4
        device = {"sub": x * 4 + to}
        return (
            pltpu.make_async_remote_copy(
                src_ref=own, dst_ref=zpatch.at[dz - 1], send_sem=z_send.at[dz - 1],
                recv_sem=z_recv.at[dz - 1], device_id=device, device_id_type=MESH,
            ),
            pltpu.make_async_remote_copy(
                src_ref=picks.at[to], dst_ref=zpick.at[dz - 1], send_sem=p_send.at[dz - 1],
                recv_sem=p_recv.at[dz - 1], device_id=device, device_id_type=MESH,
            ),
        )

    def x_copy(dx, dz):
        source = (z - dz + 4) % 4
        return pltpu.make_async_remote_copy(
            src_ref=staged.at[dx - 1, dz], dst_ref=out.at[x * 4 + source],
            send_sem=x_send.at[dx - 1, dz], recv_sem=x_recv.at[dx - 1, dz],
            device_id={"sub": (x + dx) % 4 * 4 + z}, device_id_type=MESH,
        )

    def x_arrival(dx, dz):
        origin = (x - dx + 4) % 4
        source = (z - dz + 4) % 4
        return pltpu.make_async_remote_copy(
            src_ref=staged.at[dx - 1, dz], dst_ref=out.at[origin * 4 + source],
            send_sem=x_send.at[dx - 1, dz], recv_sem=x_recv.at[dx - 1, dz],
            device_id={"sub": origin * 4 + z}, device_id_type=MESH,
        )

    for dz in (2, 1, 3):
        for copy in z_copies(dz):
            copy.start()
    for dz in (0, 1, 3, 2):
        source = (z - dz + 4) % 4
        if dz:
            for copy in z_copies(dz):
                copy.wait_recv()
            first, second, table = zpatch[dz - 1, 0], zpatch[dz - 1, 1], zpick.at[dz - 1]
        else:
            first, second, table = own[0], own[1], picks.at[z]
        for dx in (2, 1, 3, 0):
            chosen = table[pl.ds((x + dx) % 4, 1), :]
            value = jnp.where(jnp.broadcast_to(chosen, first.shape) > 0.5, second, first)
            if dx:
                staged[dx - 1, dz] = value
                x_copy(dx, dz).start()
            else:
                out[x * 4 + source] = value
    for dz in (1, 2, 3):
        for copy in z_copies(dz):
            copy.wait_send()
    for dz in (0, 1, 3, 2):
        for dx in (1, 3, 2):
            x_copy(dx, dz).wait_send()
            x_arrival(dx, dz).wait_recv()


def share_patches(own, picks):
    dma = pltpu.SemaphoreType.DMA
    return pl.pallas_call(
        patch_kernel,
        out_shape=jax.ShapeDtypeStruct((16, 64, 128), F32),
        in_specs=[VM, VM],
        out_specs=VM,
        scratch_shapes=[
            pltpu.VMEM((3, 2, 64, 128), F32),
            pltpu.VMEM((3, 8, 128), F32),
            pltpu.VMEM((3, 4, 64, 128), F32),
            dma((3,)), dma((3,)), dma((3,)), dma((3,)), dma((3, 4)), dma((3, 4)),
        ],
        compiler_params=pltpu.CompilerParams(
            collective_id=2, has_side_effects=True, vmem_limit_bytes=40 << 20
        ),
    )(own, picks)


def degrid_kernel(owners, patches, tiles, offsets, eh, el, fh, fl, out):
    low_lane = iota((64, 128), 1) < 64
    cells = iota((64, 1024), 0)

    def one(base, carry):
        patch = patches[owners[base]]
        tile = tiles[base]
        straight = patch * tile
        crossed = patch * pltpu.roll(tile, 64, 1)
        mixed = jnp.where(
            low_lane, straight - pltpu.roll(straight, 64, 1), crossed + pltpu.roll(crossed, 64, 1)
        )
        along = dot3(mixed, eh[...], el[...])
        quad = dot3(along.T, fh[...], fl[...])
        re = quad[:64, :64] - quad[64:, 64:]
        im = quad[:64, 64:] + quad[64:, :64]
        high, low = split(jnp.concatenate([re, im], 0))
        pair = jnp.concatenate([high, low], 1)
        spot = offsets[base]
        hot = jnp.where(cells == spot[0:1], 1.0, 0.0).astype(BF16)
        rows = dot(pair, jnp.concatenate([hot, hot], 0))
        hit = cells == spot[1:2]
        vis_re = jnp.sum(jnp.where(hit, rows[:64], 0.0), 0, keepdims=True)
        vis_im = jnp.sum(jnp.where(hit, rows[64:], 0.0), 0, keepdims=True)
        out[base] = jnp.concatenate([vis_re, vis_im], 0)
        return carry

    lax.fori_loop(0, 8, one, 0)


def degrid(owners, patches, tiles, offsets):
    tables = [jnp.asarray(x) for x in cell_tables()]
    return pl.pallas_call(
        degrid_kernel,
        out_shape=jax.ShapeDtypeStruct((8, 2, 1024), F32),
        in_specs=[pl.BlockSpec(memory_space=pltpu.SMEM)] + [VM] * 7,
        out_specs=VM,
        compiler_params=pltpu.CompilerParams(vmem_limit_bytes=40 << 20),
    )(owners, patches, tiles, offsets, *tables)


def local(facet_strips, taper, send_pick, bl_owner, phase_tiles, cell_offsets):
    place = jnp.stack(
        [lax.axis_index("facet"), lax.axis_index("sub"), lax.axis_index("vis")]
    ).astype(jnp.int32)
    part = strip_part(place, facet_strips[0])
    tap = taper[0].T.reshape(32, 2, 128)
    sums, windows = sum_over_facets(part.reshape(2, 4, 4, 32, 512), tap)
    window = windows.reshape(32, 16, 16).transpose(1, 0, 2).reshape(16, 512)
    own = grid_patches(sums, window)
    picks = send_pick[0, 0, 0].astype(F32).reshape(4, 4).T
    picks = jnp.broadcast_to(jnp.pad(picks, ((0, 0), (0, 4)))[:, :, None], (4, 8, 128))
    patches = share_patches(own, picks)
    result = degrid(bl_owner[0, 0, 0], patches, phase_tiles[0, 0, 0], cell_offsets[0, 0, 0])
    return result[None, None, None]


def solution(mesh):
    placed = (
        P("facet", "vis", None),
        P("sub", ("facet", "vis"), None),
        P("facet", "sub", "vis", None),
        P("facet", "sub", "vis", None),
        P("facet", "sub", "vis", None, None, None),
        P("facet", "sub", "vis", None, None, None),
    )
    return jax.shard_map(
        local,
        mesh=mesh,
        in_specs=placed,
        out_specs=P("facet", "sub", "vis", None, None, None),
        check_vma=False,
    )
```

time: 518 us -> 103 us (0.20)
  the two profiles are of different devices: /device:TPU:8 before, /device:TPU:32 now
where the time goes in v1:
time: 103 us
  Pallas kernels  98 us (95%)
  local copies, waits for them, and re-layouts  3.32 us (3%)
  other arithmetic  1.33 us (1%)
    pallas_call x1, Pallas kernels, sum_over_facets(): pl.pallas_call(sum_kernel, out_shape=(jax.ShapeDtypeStruct((32, 512), F32...  36.3 us
    pallas_call x1, Pallas kernels, grid_patches(): pl.pallas_call(grid_kernel, out_shape=jax.ShapeDtypeStruct((2, 64, 128),...  19.7 us
    pallas_call x1, Pallas kernels, share_patches(): pl.pallas_call(patch_kernel, out_shape=jax.ShapeDtypeStruct((16, 64, 128)...  17.7 us
    pallas_call x1, Pallas kernels, strip_part(): pl.pallas_call(strip_kernel, out_shape=jax.ShapeDtypeStruct((1024, 512),...  15.6 us
    pallas_call x1, Pallas kernels, degrid(): pl.pallas_call(degrid_kernel, out_shape=jax.ShapeDtypeStruct((8, 2, 1024)...  8.74 us

profile of v1, /device:TPU:32, one launch (start us, length us, event | category | flops | bytes accessed | tf_op | source)
XLA Modules:
  0.0 102.8 jit_solution(1516034943927124950)
XLA Ops:
  0.0 0.7 pad_add_fusion.place
  0.7 0.7 convert_reduce_fusion
  1.3 0.1 convert_element_type.10
  1.4 0.1 copy.24
  1.5 0.1 broadcast_in_dim.4.picks
  1.6 0.9 copy.20
  2.5 0.1 reshape.17.tap
  2.6 0.0 copy-start.1
  2.6 0.0 copy-start.2
  2.7 15.6 %shard_map.154 = f32[1024,512]{1,0:T(8,128)} custom-call(s32[3]{0:T(128)} %pad_add_fusion.place, f32[256,4096]{1,0:T(8,128)} %bitcast.20, f32[256,4096]{1,0:T(8,128)} %bitcast.21, bf16[1024,2048]{1,0:T(8,128)(2,1)} %constant.35.clone.th_ref, bf16[1024,2048]{1,0:T(8,128)(2,1)} %constant.36.clone.tl_ref, bf16[256,1024]{1,0:T(8,128)(2,1)} %constant.37.clone.lh_ref, ...), custom_call_target="tpu_custom_call" | custom-call | tf_op jit(solution)/shard_map/pallas_call | solution.py:154
  18.2 0.0 copy-start
  18.2 1.6 %copy-done = f32[1024,512]{1,0:T(8,128)S(1)} copy-done((f32[1024,512]{1,0:T(8,128)S(1)}, f32[1024,512]{1,0:T(8,128)}, u32[]{:S(2)}) %copy-start) | copy-done | bytes 2097176
  19.8 0.0 copy-start.3
  19.8 0.0 copy-start.4
  19.8 0.0 copy-start.7
  19.9 0.0 copy-start.8
  19.9 36.3 %shard_map.155 = (f32[32,512]{1,0:T(8,128)S(1)}, f32[32,2,128]{2,1,0:T(2,128)S(1)}) custom-call(f32[2,4,4,32,512]{4,3,2,1,0:T(8,128)S(1)} %bitcast.16, f32[32,2,128]{2,1,0:T(2,128)S(1)} %reshape.17.tap), custom_call_target="tpu_custom_call" | custom-call | tf_op jit(solution)/shard_map/pallas_call | solution.py:280
  56.2 0.1 copy.21
  56.3 0.1 copy.22
  56.4 0.2 reshape.19.window
  56.6 0.0 copy-done.1
  56.6 0.0 copy-done.2
  56.6 19.7 %shard_map.156.own = f32[2,64,128]{2,1,0:T(8,128)S(1)} custom-call(f32[32,512]{1,0:T(8,128)S(1)} %get-tuple-element.7.sums, f32[16,512]{1,0:T(8,128)S(1)} %reshape.19.window, bf16[512,1024]{1,0:T(8,128)(2,1)S(1)} %copy-done.2, bf16[512,1024]{1,0:T(8,128)(2,1)S(1)} %copy-done.1), custom_call_target="tpu_custom_call" | custom-call | tf_op jit(solution)/shard_map/pallas_call | solution.py:389
  76.3 17.7 %shard_map.157.patches = f32[16,64,128]{2,1,0:T(8,128)S(1)} custom-call(f32[2,64,128]{2,1,0:T(8,128)S(1)} %shard_map.156.own, f32[4,8,128]{2,1,0:T(8,128)S(1)} %broadcast_in_dim.4.picks), custom_call_target="tpu_custom_call" | custom-call | tf_op jit(solution)/shard_map/pallas_call | solution.py:481
  94.0 0.0 copy-done.9
  94.0 0.0 copy-done.3
  94.0 0.0 copy-done.4
  94.0 0.0 copy-done.5
  94.0 0.0 copy-done.6
  94.0 0.0 copy-done.7
  94.0 0.0 copy-done.8
  94.0 8.7 %shard_map.158 = f32[8,2,1024]{2,1,0:T(2,128)} custom-call(s32[8]{0:T(128)S(1)} %bitcast.19, f32[16,64,128]{2,1,0:T(8,128)S(1)} %shard_map.157.patches, f32[8,64,128]{2,1,0:T(8,128)S(1)} %bitcast.17, s32[8,2,1024]{2,1,0:T(2,128)S(1)} %bitcast.18, bf16[128,128]{1,0:T(8,128)(2,1)S(1)} %copy-done.6, bf16[128,128]{1,0:T(8,128)(2,1)S(1)} %copy-done.5, ...), custom_call_target="tpu_custom_call" | custom-call | tf_op jit(solution)/shard_map/pallas_call | solution.py:530
  (4 shorter events, 0.0 us)
Async XLA Ops:
  2.6 53.9 %copy-start.1 = (bf16[512,1024]{1,0:T(8,128)(2,1)S(1)}, bf16[512,1024]{1,0:T(8,128)(2,1)}, u32[]{:S(2)}) copy-start(bf16[512,1024]{1,0:T(8,128)(2,1)} %constant.40.clone.pw) | copy-start | bytes 3145732
  2.6 53.9 %copy-start.2 = (bf16[512,1024]{1,0:T(8,128)(2,1)S(1)}, bf16[512,1024]{1,0:T(8,128)(2,1)}, u32[]{:S(2)}) copy-start(bf16[512,1024]{1,0:T(8,128)(2,1)} %constant.39.clone.ph) | copy-start | bytes 3145732
  18.2 75.8 %copy-start.9 = (s32[1,1,1,8]{3,2,1,0:T(1,128)S(1)}, s32[1,1,1,8]{3,2,1,0:T(1,128)}, u32[]{:S(2)}) copy-start(s32[1,1,1,8]{3,2,1,0:T(1,128)} %param.19) | copy-start | bytes 100
  18.2 1.6 %copy-start = (f32[1024,512]{1,0:T(8,128)S(1)}, f32[1024,512]{1,0:T(8,128)}, u32[]{:S(2)}) copy-start(f32[1024,512]{1,0:T(8,128)} %shard_map.154) | copy-start | bytes 6291460
  19.8 74.2 %copy-start.3 = (f32[1,1,1,8,64,128]{5,4,3,2,1,0:T(8,128)S(1)}, f32[1,1,1,8,64,128]{5,4,3,2,1,0:T(8,128)}, u32[]{:S(2)}) copy-start(f32[1,1,1,8,64,128]{5,4,3,2,1,0:T(8,128)} %param.20) | copy-start | bytes 786436
  19.8 74.2 %copy-start.4 = (s32[1,1,1,8,2,1024]{5,4,3,2,1,0:T(2,128)S(1)}, s32[1,1,1,8,2,1024]{5,4,3,2,1,0:T(2,128)}, u32[]{:S(2)}) copy-start(s32[1,1,1,8,2,1024]{5,4,3,2,1,0:T(2,128)} %param.21) | copy-start | bytes 196612
  19.8 74.2 %copy-start.5 = (bf16[128,128]{1,0:T(8,128)(2,1)S(1)}, bf16[128,128]{1,0:T(8,128)(2,1)}, u32[]{:S(2)}) copy-start(bf16[128,128]{1,0:T(8,128)(2,1)} %constant.42.clone.el) | copy-start | bytes 98308
  19.8 74.2 %copy-start.6 = (bf16[128,128]{1,0:T(8,128)(2,1)S(1)}, bf16[128,128]{1,0:T(8,128)(2,1)}, u32[]{:S(2)}) copy-start(bf16[128,128]{1,0:T(8,128)(2,1)} %constant.41.clone.eh) | copy-start | bytes 98308
  19.8 74.2 %copy-start.7 = (bf16[64,128]{1,0:T(8,128)(2,1)S(1)}, bf16[64,128]{1,0:T(8,128)(2,1)}, u32[]{:S(2)}) copy-start(bf16[64,128]{1,0:T(8,128)(2,1)} %constant.44.clone.fl) | copy-start | bytes 49156
  19.9 74.2 %copy-start.8 = (bf16[64,128]{1,0:T(8,128)(2,1)S(1)}, bf16[64,128]{1,0:T(8,128)(2,1)}, u32[]{:S(2)}) copy-start(bf16[64,128]{1,0:T(8,128)(2,1)} %constant.43.clone.fh) | copy-start | bytes 49156

commit v2 on v1

v2 whole, which is shorter than its diff:
```python
import functools
import math

import jax
import jax.numpy as jnp
import ml_dtypes
import numpy as np
from jax import lax
from jax.experimental import pallas as pl
from jax.experimental.pallas import tpu as pltpu
from jax.sharding import PartitionSpec as P

MESH = pl.DeviceIdType.MESH
F32 = jnp.float32
BF16 = jnp.bfloat16
VM = pl.BlockSpec(memory_space=pltpu.VMEM)
SCALE = 1.0 / math.sqrt(512 * 2048 * 16)


def halves(table):
    high = table.astype(np.float32).astype(ml_dtypes.bfloat16)
    low = (table - high.astype(np.float64)).astype(ml_dtypes.bfloat16)
    return high, low


@functools.lru_cache(None)
def column_table():
    freq = np.arange(512).reshape(2, 4, 4, 16).transpose(2, 0, 1, 3).reshape(4, 1, 128)
    cols = np.arange(2048)[None, :, None]
    angle = (33 * freq * cols % 65536) * (2.0 * np.pi / 65536)
    return halves(np.concatenate([np.cos(angle), -np.sin(angle)], 2))


@functools.lru_cache(None)
def row_table():
    rows = np.arange(256)[:, None]
    freq = np.arange(512)[None, :]
    angle = (257 * freq * rows % 65536) * (2.0 * np.pi / 65536)
    return halves(np.concatenate([np.cos(angle), -np.sin(angle)], 1))


@functools.lru_cache(None)
def grid_table():
    left = np.arange(512)[:, None]
    right = np.arange(512)[None, :]
    angle = (left * right % 512) * (2.0 * np.pi / 512)
    scale = 1.0 / math.sqrt(512)
    both = np.stack(
        [np.cos(angle).reshape(512, 8, 64) * scale, np.sin(angle).reshape(512, 8, 64) * scale], 2
    )
    return halves(both.reshape(512, 1024))


@functools.lru_cache(None)
def cell_tables():
    left = np.arange(64)[:, None]
    right = np.arange(64)[None, :]
    angle = (left * right % 64) * (2.0 * np.pi / 64)
    cos, sin = np.cos(angle) / 8.0, -np.sin(angle) / 8.0
    square = np.concatenate(
        [np.concatenate([cos, sin], 1), np.concatenate([-sin, cos], 1)], 0
    )
    flat = np.concatenate([cos, sin], 1)
    return halves(square) + halves(flat)


def split(value):
    high = value.astype(BF16)
    return high, (value - high.astype(F32)).astype(BF16)


def dot(left, right):
    return jnp.dot(left, right, preferred_element_type=F32)


def dot_t(left, right):
    return lax.dot_general(left, right, (((1,), (1,)), ((), ())), preferred_element_type=F32)


def dot3(left, right_high, right_low):
    high, low = split(left)
    return dot(high, right_high) + dot(low, right_high) + dot(high, right_low)


def turned(turns, modulus):
    angles = (turns & (modulus - 1)).astype(F32) * (2.0 * math.pi / modulus)
    return jnp.cos(angles), -jnp.sin(angles)


def iota(shape, dim):
    return lax.broadcasted_iota(jnp.int32, shape, dim)


def here():
    facet, sub, core = lax.axis_index("facet"), lax.axis_index("sub"), lax.axis_index("vis")
    return facet // 4, facet % 4, sub // 4, sub % 4, core


def swapped(top, bottom):
    sign = jnp.where(iota(top.shape, 1) < 64, -1.0, 1.0).astype(F32)
    return top + pltpu.roll(bottom, 64, 1) * sign


PIECES = 4
near = [(dy, dc) for dy in range(4) for dc in range(2) if dy or dc]


def remote(src, dst, send, recv, device):
    return pltpu.make_async_remote_copy(
        src_ref=src, dst_ref=dst, send_sem=send, recv_sem=recv,
        device_id=device, device_id_type=MESH,
    )


def placed_taper(blocks):
    values = jnp.concatenate([blocks[:, 0, :], blocks[:, 1, :]], 1).T
    high = values.astype(BF16)
    middle, low = split(values - high.astype(F32))
    spread = jnp.where(iota((32, 512), 1) // 16 == iota((32, 512), 0), 1.0, 0.0).astype(BF16)
    wide = dot(high, spread) + (dot(middle, spread) + dot(low, spread))
    hit = (iota((256, 512), 0) & 15) == (iota((256, 512), 1) & 15)
    return jnp.sum(jnp.where(hit, wide, 0.0).reshape(16, 16, 512), 1)


def patch_kernel(
    strip, th_hbm, tl_hbm, lh_ref, ll_ref, tap, ph, pw, pick_ref, out,
    raw, xh, xl, th, tl, part, got_core, got_y, tot, got_z, tap_out,
    ubuf, zbuf, ybuf, own, picks, zpatch, zpick, staged,
    raw_sem, t_sem, core_send, core_recv, y_send, y_recv, z_send, z_recv, tap_send, tap_recv,
    uz_send, uz_recv, uy_send, uy_recv, w_send, w_recv, p_send, p_recv, x_send, x_recv,
):
    z, y, x, w, c = here()
    facet, sub, core = lax.axis_index("facet"), lax.axis_index("sub"), c
    me = (z * 4 + y) * 2 + c
    width = 2048 // PIECES
    order = (2, 1, 3, 0)

    def raw_copy(index):
        where = pl.ds(index * width, width)
        return pltpu.make_async_copy(strip.at[:, where], raw.at[:, where], raw_sem.at[index])

    def t_copies(dz):
        at = (z + dz) % 4
        return (
            pltpu.make_async_copy(th_hbm.at[at], th.at[dz], t_sem.at[dz, 0]),
            pltpu.make_async_copy(tl_hbm.at[at], tl.at[dz], t_sem.at[dz, 1]),
        )

    for index in range(PIECES):
        raw_copy(index).start()
        raw_copy(index + PIECES).start()
        if index == 0:
            for copy in t_copies(order[0]):
                copy.start()
    for dz in order[1:]:
        for copy in t_copies(dz):
            copy.start()

    barrier = pltpu.get_barrier_semaphore()

    def greet(step, carry):
        peer = (me + step) % 32
        pl.semaphore_signal(
            barrier, inc=1, device_id={"facet": peer // 2, "vis": peer % 2}, device_id_type=MESH
        )
        return carry

    lax.fori_loop(1, 32, greet, 0)
    for step in (1, 2, 3):
        pl.semaphore_signal(
            barrier, inc=1, device_id={"sub": x * 4 + (w + step) % 4}, device_id_type=MESH
        )
        pl.semaphore_signal(
            barrier, inc=1, device_id={"sub": (x + step) % 4 * 4 + w}, device_id_type=MESH
        )

    def core_copy(dz):
        return remote(
            part.at[dz, 1 - c], got_core.at[dz], core_send.at[dz], core_recv.at[dz], {"vis": 1 - c}
        )

    def y_copy(dz, dy):
        to = (y + dy) % 4
        return remote(
            part.at[dz, c, to], got_y.at[dz, dy - 1], y_send.at[dz, dy - 1],
            y_recv.at[dz, dy - 1], {"facet": z * 4 + to},
        )

    def z_copy(dz):
        return remote(
            tot.at[dz], got_z.at[dz - 1], z_send.at[dz - 1], z_recv.at[dz - 1],
            {"facet": (z + dz) % 4 * 4 + y},
        )

    def tap_copy(step):
        peer = (me + step) % 32
        block = (peer % 2) * 16 + (peer // 2 % 4) * 4 + peer // 8
        return remote(
            tap.at[block], tap_out.at[me], tap_send.at[step], tap_recv.at[step],
            {"facet": peer // 2, "vis": peer % 2},
        )

    def tap_arrival(step):
        source = (me - step + 32) % 32
        return remote(
            tap.at[0], tap_out.at[source], tap_send.at[step], tap_recv.at[step],
            {"facet": source // 2, "vis": source % 2},
        )

    def after_core(dz):
        core_copy(dz).wait()
        part[dz, c] = part[dz, c] + got_core[dz]
        for dy in (2, 1, 3):
            y_copy(dz, dy).start()

    def after_y(dz):
        for dy in (1, 3, 2):
            y_copy(dz, dy).wait()
        tot[dz] = (part[dz, c, y] + got_y[dz, 0]) + (got_y[dz, 1] + got_y[dz, 2])
        if dz:
            z_copy(dz).start()

    rows = core * 256 + iota((8, 256), 1)
    r_re, r_im = turned(sub * 4099 * rows, 65536)
    r_re, r_im = r_re[0:1], r_im[0:1]
    freq = iota((16, 512), 1)
    other = iota((16, 512), 0)
    turn = facet * ((freq + 5 * other + 6 * sub) & 15) * 16 + freq * core
    w_re, w_im = turned(turn, 256)
    w_re, w_im = (w_re * SCALE)[None], (w_im * SCALE)[None]

    def finish(dz, acc):
        top, bottom = acc[:256], acc[256:]
        a_re = (top[:, :128] - bottom[:, 128:]).T
        a_im = (top[:, 128:] + bottom[:, :128]).T
        both = jnp.concatenate([a_re * r_re - a_im * r_im, a_re * r_im + a_im * r_re], 0)
        prod = dot3(both, lh_ref[...], ll_ref[...])
        p_re, p_im = prod[:128], prod[128:]
        o_re = (p_re[:, :512] - p_im[:, 512:]).reshape(8, 16, 512)
        o_im = (p_re[:, 512:] + p_im[:, :512]).reshape(8, 16, 512)
        part[dz, :, :, 0:16, :] = (o_re * w_re - o_im * w_im).reshape(2, 4, 16, 512)
        part[dz, :, :, 16:32, :] = (o_re * w_im + o_im * w_re).reshape(2, 4, 16, 512)
        core_copy(dz).start()

    def multiply(dz, where):
        high, low = xh[:, where], xl[:, where]
        t_high, t_low = th[dz, where, :], tl[dz, where, :]
        return dot(high, t_high) + dot(low, t_high) + dot(high, t_low)

    picks[...] = jnp.zeros_like(picks)
    for other_z in range(4):
        for other_x in range(4):
            value = pick_ref[other_x * 4 + other_z].astype(F32)
            picks[other_z, other_x : other_x + 1, :] = jnp.full((1, 128), value, F32)

    acc = None
    for index in range(PIECES):
        raw_copy(index).wait()
        raw_copy(index + PIECES).wait()
        where = slice(index * width, index * width + width)
        cols = index * width + iota((8, width), 1)
        c_re, c_im = turned(sub * 1031 * cols, 65536)
        c_re, c_im = c_re[0:1], c_im[0:1]
        s_re, s_im = raw[:, where], raw[:, slice(2048 + where.start, 2048 + where.stop)]
        for half, moved in enumerate((s_re * c_re - s_im * c_im, s_re * c_im + s_im * c_re)):
            high, low = split(moved)
            xh[half * 256 : half * 256 + 256, where] = high
            xl[half * 256 : half * 256 + 256, where] = low
        if index == 0:
            for copy in t_copies(order[0]):
                copy.wait()
        more = multiply(order[0], where)
        acc = more if acc is None else acc + more
    pl.semaphore_wait(barrier, 37)
    finish(2, acc)

    def tap_start(step, carry):
        tap_copy(step).start()
        return carry

    lax.fori_loop(1, 32, tap_start, 0)
    tap_out[me] = tap[c * 16 + y * 4 + z]

    def chunk(dz, between):
        for copy in t_copies(dz):
            copy.wait()
        acc = multiply(dz, slice(0, 1024))
        between()
        finish(dz, acc + multiply(dz, slice(1024, 2048)))

    chunk(1, lambda: after_core(2))

    def between_three():
        after_core(1)
        after_y(2)

    chunk(3, between_three)

    def between_four():
        after_core(3)
        after_y(1)

    chunk(0, between_four)
    after_core(0)
    after_y(3)

    def tap_wait(step, carry):
        tap_copy(step).wait_send()
        tap_arrival(step).wait_recv()
        return carry

    lax.fori_loop(1, 32, tap_wait, 0)
    taper = placed_taper(tap_out[...])
    after_y(0)
    for dz in (2, 1, 3):
        z_copy(dz).wait()
    sums = (tot[0] + got_z[0]) + (got_z[1] + got_z[2])

    tapered = sums * jnp.concatenate([taper, taper], 0)
    prod = dot3(tapered, ph[...], pw[...])
    for block in range(8):
        where = slice(block * 128, block * 128 + 128)
        ubuf[block // 2, block % 2] = swapped(prod[:16, where], prod[16:, where])

    def uz_copy(dz):
        to = (z + dz) % 4
        return remote(
            ubuf.at[to], zbuf.at[z], uz_send.at[dz - 1], uz_recv.at[dz - 1], {"facet": to * 4 + y}
        )

    def uz_arrival(dz):
        source = (z - dz + 4) % 4
        return remote(
            ubuf.at[source], zbuf.at[source], uz_send.at[dz - 1], uz_recv.at[dz - 1],
            {"facet": source * 4 + y},
        )

    def uy_copy(index):
        dy, dc = near[index]
        to = (y + dy) % 4
        return remote(
            zbuf.at[:, to // 2], ybuf.at[c, y], uy_send.at[index], uy_recv.at[index],
            {"facet": z * 4 + to, "vis": (c + dc) % 2},
        )

    def uy_arrival(index):
        dy, dc = near[index]
        source = (y - dy + 4) % 4
        return remote(
            zbuf.at[:, 0], ybuf.at[(c + dc) % 2, source], uy_send.at[index], uy_recv.at[index],
            {"facet": z * 4 + source, "vis": (c + dc) % 2},
        )

    for dz in (2, 1, 3):
        uz_copy(dz).start()
    zbuf[z] = ubuf[z]
    for dz in (1, 3, 2):
        uz_arrival(dz).wait_recv()
    for index in range(7):
        uy_copy(index).start()
    ybuf[c, y] = zbuf[:, y // 2]
    for dz in (1, 2, 3):
        uz_copy(dz).wait_send()
    for index in range(7):
        uy_copy(index).wait_send()
        uy_arrival(index).wait_recv()
    cols = ybuf[...].reshape(512, 128).T
    where = pl.ds(pl.multiple_of(((y % 2) * 2 + c) * 256, 256), 256)
    prod = dot3(cols, ph[:, where], pw[:, where])
    for j in range(2):
        where = slice(j * 128, j * 128 + 128)
        own[j] = swapped(prod[:64, where], prod[64:, where])

    def w_copies(dz):
        to = (w + dz) % 4
        device = {"sub": x * 4 + to}
        return (
            remote(own, zpatch.at[dz - 1], w_send.at[dz - 1], w_recv.at[dz - 1], device),
            remote(picks.at[to], zpick.at[dz - 1], p_send.at[dz - 1], p_recv.at[dz - 1], device),
        )

    def x_copy(dx, dz):
        source = (w - dz + 4) % 4
        return remote(
            staged.at[dx - 1, dz], out.at[x * 4 + source], x_send.at[dx - 1, dz],
            x_recv.at[dx - 1, dz], {"sub": (x + dx) % 4 * 4 + w},
        )

    def x_arrival(dx, dz):
        origin = (x - dx + 4) % 4
        source = (w - dz + 4) % 4
        return remote(
            staged.at[dx - 1, dz], out.at[origin * 4 + source], x_send.at[dx - 1, dz],
            x_recv.at[dx - 1, dz], {"sub": origin * 4 + w},
        )

    for dz in (2, 1, 3):
        for copy in w_copies(dz):
            copy.start()
    for dz in (0, 1, 3, 2):
        source = (w - dz + 4) % 4
        if dz:
            for copy in w_copies(dz):
                copy.wait_recv()
            first, second, table = zpatch[dz - 1, 0], zpatch[dz - 1, 1], zpick.at[dz - 1]
        else:
            first, second, table = own[0], own[1], picks.at[w]
        for dx in (2, 1, 3, 0):
            chosen = table[pl.ds((x + dx) % 4, 1), :]
            value = jnp.where(jnp.broadcast_to(chosen, first.shape) > 0.5, second, first)
            if dx:
                staged[dx - 1, dz] = value
                x_copy(dx, dz).start()
            else:
                out[x * 4 + source] = value
    for dz in (1, 2, 3):
        for copy in w_copies(dz):
            copy.wait_send()
    for dz in (0, 1, 3, 2):
        for dx in (1, 3, 2):
            x_copy(dx, dz).wait_send()
            x_arrival(dx, dz).wait_recv()


def shared_patches(strip, tap, pick_row):
    dma = pltpu.SemaphoreType.DMA
    tables = [jnp.asarray(x) for x in column_table() + row_table()]
    ph, pw = (jnp.asarray(x) for x in grid_table())
    far = pl.BlockSpec(memory_space=pl.ANY)
    return pl.pallas_call(
        patch_kernel,
        out_shape=jax.ShapeDtypeStruct((16, 64, 128), F32),
        in_specs=[far] * 3 + [VM] * 5 + [pl.BlockSpec(memory_space=pltpu.SMEM)],
        out_specs=VM,
        scratch_shapes=[
            pltpu.VMEM((256, 4096), F32),
            pltpu.VMEM((512, 2048), BF16),
            pltpu.VMEM((512, 2048), BF16),
            pltpu.VMEM((4, 2048, 256), BF16),
            pltpu.VMEM((4, 2048, 256), BF16),
            pltpu.VMEM((4, 2, 4, 32, 512), F32),
            pltpu.VMEM((4, 4, 32, 512), F32),
            pltpu.VMEM((4, 3, 32, 512), F32),
            pltpu.VMEM((4, 32, 512), F32),
            pltpu.VMEM((3, 32, 512), F32),
            pltpu.VMEM((32, 2, 128), F32),
            pltpu.VMEM((4, 2, 16, 128), F32),
            pltpu.VMEM((4, 2, 16, 128), F32),
            pltpu.VMEM((2, 4, 4, 16, 128), F32),
            pltpu.VMEM((2, 64, 128), F32),
            pltpu.VMEM((4, 8, 128), F32),
            pltpu.VMEM((3, 2, 64, 128), F32),
            pltpu.VMEM((3, 8, 128), F32),
            pltpu.VMEM((3, 4, 64, 128), F32),
            dma((2 * PIECES,)), dma((4, 2)),
            dma((4,)), dma((4,)), dma((4, 3)), dma((4, 3)), dma((3,)), dma((3,)),
            dma((32,)), dma((32,)),
            dma((3,)), dma((3,)), dma((7,)), dma((7,)),
            dma((3,)), dma((3,)), dma((3,)), dma((3,)), dma((3, 4)), dma((3, 4)),
        ],
        compiler_params=pltpu.CompilerParams(
            collective_id=0, has_side_effects=True, vmem_limit_bytes=58 << 20
        ),
    )(strip, *tables, tap, ph, pw, pick_row)


def degrid_kernel(owners, patches, tiles, offsets, eh, el, fh, fl, out):
    low_lane = iota((64, 128), 1) < 64
    cells = iota((64, 1024), 0)

    def one(base, carry):
        patch = patches[owners[base]]
        tile = tiles[base]
        straight = patch * tile
        crossed = patch * pltpu.roll(tile, 64, 1)
        mixed = jnp.where(
            low_lane, straight - pltpu.roll(straight, 64, 1), crossed + pltpu.roll(crossed, 64, 1)
        )
        along = dot3(mixed, eh[...], el[...])
        quad = dot3(along.T, fh[...], fl[...])
        re = quad[:64, :64] - quad[64:, 64:]
        im = quad[:64, 64:] + quad[64:, :64]
        high, low = split(jnp.concatenate([re, im], 0))
        pair = jnp.concatenate([high, low], 1)
        spot = offsets[base]
        hot = jnp.where(cells == spot[0:1], 1.0, 0.0).astype(BF16)
        rows = dot(pair, jnp.concatenate([hot, hot], 0))
        hit = cells == spot[1:2]
        vis_re = jnp.sum(jnp.where(hit, rows[:64], 0.0), 0, keepdims=True)
        vis_im = jnp.sum(jnp.where(hit, rows[64:], 0.0), 0, keepdims=True)
        out[base] = jnp.concatenate([vis_re, vis_im], 0)
        return carry

    lax.fori_loop(0, 8, one, 0, unroll=True)


def degrid(owners, patches, tiles, offsets):
    tables = [jnp.asarray(x) for x in cell_tables()]
    return pl.pallas_call(
        degrid_kernel,
        out_shape=jax.ShapeDtypeStruct((8, 2, 1024), F32),
        in_specs=[pl.BlockSpec(memory_space=pltpu.SMEM)] + [VM] * 7,
        out_specs=VM,
        compiler_params=pltpu.CompilerParams(vmem_limit_bytes=40 << 20),
    )(owners, patches, tiles, offsets, *tables)


def local(facet_strips, taper, send_pick, bl_owner, phase_tiles, cell_offsets):
    tap = taper[0].T.reshape(32, 2, 128)
    patches = shared_patches(facet_strips[0], tap, send_pick[0, 0, 0])
    result = degrid(bl_owner[0, 0, 0], patches, phase_tiles[0, 0, 0], cell_offsets[0, 0, 0])
    return result[None, None, None]


def solution(mesh):
    placed = (
        P("facet", "vis", None),
        P("sub", ("facet", "vis"), None),
        P("facet", "sub", "vis", None),
        P("facet", "sub", "vis", None),
        P("facet", "sub", "vis", None, None, None),
        P("facet", "sub", "vis", None, None, None),
    )
    return jax.shard_map(
        local,
        mesh=mesh,
        in_specs=placed,
        out_specs=P("facet", "sub", "vis", None, None, None),
        check_vma=False,
    )
```

time: 103 us -> 83.6 us (0.81)
  Pallas kernels: 98 us -> 80.5 us
  other arithmetic: 1.33 us -> 0 us
    pallas_call x4 -> x1, Pallas kernels: 89.2 us -> 73.4 us  [shared_patches(): pl.pallas_call(patch_kernel, out_shape=jax.ShapeDtypeStruct((16, 64, 128)...]
    pallas_call x1, Pallas kernels: 8.74 us -> 7.09 us  [degrid(): pl.pallas_call(degrid_kernel, out_shape=jax.ShapeDtypeStruct((8, 2, 1024)...]
where the time goes in v2:
time: 83.6 us; the launch traced here: 83.3 us
  Pallas kernels  80.5 us (96%)
  local copies, waits for them, and re-layouts  2.71 us (3%)
    pallas_call x1, Pallas kernels, shared_patches(): pl.pallas_call(patch_kernel, out_shape=jax.ShapeDtypeStruct((16, 64, 128)...  73.4 us
    pallas_call x1, Pallas kernels, degrid(): pl.pallas_call(degrid_kernel, out_shape=jax.ShapeDtypeStruct((8, 2, 1024)...  7.09 us

profile of v2, /device:TPU:32, one launch (start us, length us, event | category | flops | bytes accessed | tf_op | source)
XLA Modules:
  0.0 83.3 jit_solution(8165553784560962765)
XLA Ops:
  0.0 0.9 %copy.18 = f32[512,16]{1,0:T(8,128)S(1)} copy(f32[512,16]{0,1:T(8,128)} %bitcast.13) | data formatting | bytes 65536 | tf_op jit(solution)/shard_map/transpose | solution.py:509
  0.9 0.8 reshape.3.tap
  1.6 0.0 copy-start.1
  1.6 0.0 copy-start.2
  1.7 0.0 copy-start.3
  1.7 0.0 copy-start.4
  1.7 0.0 copy-start.5
  1.7 0.0 copy-start.6
  1.7 0.0 copy-start.7
  1.7 73.4 %shard_map.154.patches = f32[16,64,128]{2,1,0:T(8,128)} custom-call(f32[256,4096]{1,0:T(8,128)} %bitcast.12, bf16[4,2048,256]{2,1,0:T(8,128)(2,1)} %constant.20.clone.th_hbm, bf16[4,2048,256]{2,1,0:T(8,128)(2,1)} %constant.21.clone.tl_hbm, bf16[256,1024]{1,0:T(8,128)(2,1)} %constant.22.clone.lh_ref, bf16[256,1024]{1,0:T(8,128)(2,1)} %constant.23.clone.ll_ref, ...), custom_call_target="tpu_custom_call" | custom-call | tf_op jit(solution)/shard_map/pallas_call | solution.py:430
  75.1 0.0 copy-done.1
  75.2 0.0 copy-done.2
  75.2 0.0 copy-done.3
  75.2 0.0 copy-done.4
  75.2 0.0 copy-done.5
  75.2 0.0 copy-done.6
  75.2 0.0 copy-done.7
  75.2 0.0 copy-start
  75.2 1.0 %copy-done = f32[16,64,128]{2,1,0:T(8,128)S(1)} copy-done((f32[16,64,128]{2,1,0:T(8,128)S(1)}, f32[16,64,128]{2,1,0:T(8,128)}, u32[]{:S(2)}) %copy-start) | copy-done | bytes 524312
  76.3 7.1 %shard_map.155 = f32[8,2,1024]{2,1,0:T(2,128)} custom-call(s32[8]{0:T(128)S(1)} %bitcast.11, f32[16,64,128]{2,1,0:T(8,128)S(1)} %copy-done, f32[8,64,128]{2,1,0:T(8,128)S(1)} %bitcast.9, s32[8,2,1024]{2,1,0:T(2,128)S(1)} %bitcast.10, bf16[128,128]{1,0:T(8,128)(2,1)S(1)} %copy-done.4, bf16[128,128]{1,0:T(8,128)(2,1)S(1)} %copy-done.3, ...), custom_call_target="tpu_custom_call" | custom-call | tf_op jit(solution)/shard_map/pallas_call | solution.py:499
Async XLA Ops:
  1.6 73.5 %copy-start.1 = (f32[1,1,1,8,64,128]{5,4,3,2,1,0:T(8,128)S(1)}, f32[1,1,1,8,64,128]{5,4,3,2,1,0:T(8,128)}, u32[]{:S(2)}) copy-start(f32[1,1,1,8,64,128]{5,4,3,2,1,0:T(8,128)} %param.20) | copy-start | bytes 786436
  1.6 73.5 %copy-start.2 = (s32[1,1,1,8,2,1024]{5,4,3,2,1,0:T(2,128)S(1)}, s32[1,1,1,8,2,1024]{5,4,3,2,1,0:T(2,128)}, u32[]{:S(2)}) copy-start(s32[1,1,1,8,2,1024]{5,4,3,2,1,0:T(2,128)} %param.21) | copy-start | bytes 196612
  1.7 73.5 %copy-start.3 = (bf16[128,128]{1,0:T(8,128)(2,1)S(1)}, bf16[128,128]{1,0:T(8,128)(2,1)}, u32[]{:S(2)}) copy-start(bf16[128,128]{1,0:T(8,128)(2,1)} %constant.27.clone.el) | copy-start | bytes 98308
  1.7 73.5 %copy-start.4 = (bf16[128,128]{1,0:T(8,128)(2,1)S(1)}, bf16[128,128]{1,0:T(8,128)(2,1)}, u32[]{:S(2)}) copy-start(bf16[128,128]{1,0:T(8,128)(2,1)} %constant.26.clone.eh) | copy-start | bytes 98308
  1.7 73.5 %copy-start.5 = (bf16[64,128]{1,0:T(8,128)(2,1)S(1)}, bf16[64,128]{1,0:T(8,128)(2,1)}, u32[]{:S(2)}) copy-start(bf16[64,128]{1,0:T(8,128)(2,1)} %constant.29.clone.fl) | copy-start | bytes 49156
  1.7 73.5 %copy-start.6 = (bf16[64,128]{1,0:T(8,128)(2,1)S(1)}, bf16[64,128]{1,0:T(8,128)(2,1)}, u32[]{:S(2)}) copy-start(bf16[64,128]{1,0:T(8,128)(2,1)} %constant.28.clone.fh) | copy-start | bytes 49156
  1.7 73.5 %copy-start.7 = (s32[1,1,1,8]{3,2,1,0:T(1,128)S(1)}, s32[1,1,1,8]{3,2,1,0:T(1,128)}, u32[]{:S(2)}) copy-start(s32[1,1,1,8]{3,2,1,0:T(1,128)} %param.19) | copy-start | bytes 100
  75.2 1.0 %copy-start = (f32[16,64,128]{2,1,0:T(8,128)S(1)}, f32[16,64,128]{2,1,0:T(8,128)}, u32[]{:S(2)}) copy-start(f32[16,64,128]{2,1,0:T(8,128)} %shard_map.154.patches) | copy-start | bytes 1572868

commit v3 on v2

--- a/solution.py
+++ b/solution.py
@@ -23,12 +23,19 @@
     return high, low
 
 
+PIECES = 4
+WIDTH = 2048 // PIECES
+
+
 @functools.lru_cache(None)
 def column_table():
     freq = np.arange(512).reshape(2, 4, 4, 16).transpose(2, 0, 1, 3).reshape(4, 1, 128)
     cols = np.arange(2048)[None, :, None]
     angle = (33 * freq * cols % 65536) * (2.0 * np.pi / 65536)
-    return halves(np.concatenate([np.cos(angle), -np.sin(angle)], 2))
+    cos, sin = np.cos(angle), -np.sin(angle)
+    top = np.concatenate([cos, sin], 2).reshape(4, PIECES, 1, WIDTH, 256)
+    bottom = np.concatenate([-sin, cos], 2).reshape(4, PIECES, 1, WIDTH, 256)
+    return halves(np.concatenate([top, bottom], 2).reshape(4, 4096, 256))
 
 
 @functools.lru_cache(None)
@@ -36,7 +43,9 @@
     rows = np.arange(256)[:, None]
     freq = np.arange(512)[None, :]
     angle = (257 * freq * rows % 65536) * (2.0 * np.pi / 65536)
-    return halves(np.concatenate([np.cos(angle), -np.sin(angle)], 1))
+    cos, sin = np.cos(angle), -np.sin(angle)
+    top, bottom = np.concatenate([cos, sin], 1), np.concatenate([-sin, cos], 1)
+    return halves(np.concatenate([top, bottom], 0))
 
 
 @functools.lru_cache(None)
@@ -101,7 +110,6 @@
     return top + pltpu.roll(bottom, 64, 1) * sign
 
 
-PIECES = 4
 near = [(dy, dc) for dy in range(4) for dc in range(2) if dy or dc]
 
 
@@ -112,32 +120,50 @@
     )
 
 
+def exact(left, chosen):
+    high = left.astype(BF16)
+    middle, low = split(left - high.astype(F32))
+    return dot(high, chosen) + (dot(middle, chosen) + dot(low, chosen))
+
+
+def ones_where(condition):
+    return jnp.where(condition, 1.0, 0.0).astype(BF16)
+
+
+def cut_taper(rows):
+    wide = exact(rows.T, ones_where((iota((16, 256), 1) & 15) == iota((16, 256), 0)))
+    hit = (iota((512, 256), 0) & 15) == iota((512, 256), 1) // 16
+    return jnp.sum(jnp.where(hit, wide, 0.0).reshape(32, 16, 256), 1)
+
+
 def placed_taper(blocks):
     values = jnp.concatenate([blocks[:, 0, :], blocks[:, 1, :]], 1).T
-    high = values.astype(BF16)
-    middle, low = split(values - high.astype(F32))
-    spread = jnp.where(iota((32, 512), 1) // 16 == iota((32, 512), 0), 1.0, 0.0).astype(BF16)
-    wide = dot(high, spread) + (dot(middle, spread) + dot(low, spread))
+    wide = exact(values, ones_where(iota((32, 512), 1) // 16 == iota((32, 512), 0)))
     hit = (iota((256, 512), 0) & 15) == (iota((256, 512), 1) & 15)
     return jnp.sum(jnp.where(hit, wide, 0.0).reshape(16, 16, 512), 1)
 
 
 def patch_kernel(
-    strip, th_hbm, tl_hbm, lh_ref, ll_ref, tap, ph, pw, pick_ref, out,
-    raw, xh, xl, th, tl, part, got_core, got_y, tot, got_z, tap_out,
+    strip, th_hbm, tl_hbm, lh_ref, ll_ref, window, ph, pw, pick_ref, out,
+    tap, acc, raw, xh, xl, th, tl, part, got_core, got_y, tot, got_far, got_z, tap_out,
     ubuf, zbuf, ybuf, own, picks, zpatch, zpick, staged,
-    raw_sem, t_sem, core_send, core_recv, y_send, y_recv, z_send, z_recv, tap_send, tap_recv,
+    raw_sem, t_sem, core_send, core_recv, y_send, y_recv, far_send, far_recv, z_send, z_recv, tap_send, tap_recv,
     uz_send, uz_recv, uy_send, uy_recv, w_send, w_recv, p_send, p_recv, x_send, x_recv,
 ):
     z, y, x, w, c = here()
     facet, sub, core = lax.axis_index("facet"), lax.axis_index("sub"), c
     me = (z * 4 + y) * 2 + c
-    width = 2048 // PIECES
     order = (2, 1, 3, 0)
 
-    def raw_copy(index):
-        where = pl.ds(index * width, width)
-        return pltpu.make_async_copy(strip.at[:, where], raw.at[:, where], raw_sem.at[index])
+    def piece_copies(index):
+        re, im = pl.ds(index * WIDTH, WIDTH), pl.ds(2048 + index * WIDTH, WIDTH)
+        rows, at = pl.ds(index * 2 * WIDTH, 2 * WIDTH), (z + order[0]) % 4
+        return (
+            pltpu.make_async_copy(strip.at[:, re], raw.at[:, re], raw_sem.at[index, 0]),
+            pltpu.make_async_copy(strip.at[:, im], raw.at[:, im], raw_sem.at[index, 1]),
+            pltpu.make_async_copy(th_hbm.at[at, rows], th.at[order[0], rows], raw_sem.at[index, 2]),
+            pltpu.make_async_copy(tl_hbm.at[at, rows], tl.at[order[0], rows], raw_sem.at[index, 3]),
+        )
 
     def t_copies(dz):
         at = (z + dz) % 4
@@ -147,15 +173,8 @@
         )
 
     for index in range(PIECES):
-        raw_copy(index).start()
-        raw_copy(index + PIECES).start()
-        if index == 0:
-            for copy in t_copies(order[0]):
-                copy.start()
-    for dz in order[1:]:
-        for copy in t_copies(dz):
+        for copy in piece_copies(index):
             copy.start()
-
     barrier = pltpu.get_barrier_semaphore()
 
     def greet(step, carry):
@@ -186,10 +205,19 @@
             y_recv.at[dz, dy - 1], {"facet": z * 4 + to},
         )
 
-    def z_copy(dz):
-        return remote(
-            tot.at[dz], got_z.at[dz - 1], z_send.at[dz - 1], z_recv.at[dz - 1],
-            {"facet": (z + dz) % 4 * 4 + y},
+    up_z, down_z = {"facet": (z + 1) % 4 * 4 + y}, {"facet": (z + 3) % 4 * 4 + y}
+    first, last = pl.ds(0, 16), pl.ds(16, 16)
+
+    def far_copy(side):
+        return remote(
+            tot.at[2, last if side else first], got_far.at[side], far_send.at[side],
+            far_recv.at[side], down_z if side else up_z,
+        )
+
+    def z_copy(side):
+        return remote(
+            tot.at[1 + 2 * side], got_z.at[side], z_send.at[side], z_recv.at[side],
+            down_z if side else up_z,
         )
 
     def tap_copy(step):
@@ -217,8 +245,15 @@
         for dy in (1, 3, 2):
             y_copy(dz, dy).wait()
         tot[dz] = (part[dz, c, y] + got_y[dz, 0]) + (got_y[dz, 1] + got_y[dz, 2])
-        if dz:
-            z_copy(dz).start()
+        if dz == 2:
+            far_copy(0).start()
+            far_copy(1).start()
+
+    def after_far(side):
+        far_copy(side).wait()
+        half, dz = (last, 3) if side else (first, 1)
+        tot[dz, half] = tot[dz, half] + got_far[side]
+        z_copy(side).start()
 
     rows = core * 256 + iota((8, 256), 1)
     r_re, r_im = turned(sub * 4099 * rows, 65536)
@@ -229,50 +264,63 @@
     w_re, w_im = turned(turn, 256)
     w_re, w_im = (w_re * SCALE)[None], (w_im * SCALE)[None]
 
-    def finish(dz, acc):
-        top, bottom = acc[:256], acc[256:]
-        a_re = (top[:, :128] - bottom[:, 128:]).T
-        a_im = (top[:, 128:] + bottom[:, :128]).T
-        both = jnp.concatenate([a_re * r_re - a_im * r_im, a_re * r_im + a_im * r_re], 0)
+    def finish(dz):
+        turned_acc = acc[...].T
+        a_re, a_im = turned_acc[:128], turned_acc[128:]
+        both = jnp.concatenate([a_re * r_re - a_im * r_im, a_re * r_im + a_im * r_re], 1)
         prod = dot3(both, lh_ref[...], ll_ref[...])
-        p_re, p_im = prod[:128], prod[128:]
-        o_re = (p_re[:, :512] - p_im[:, 512:]).reshape(8, 16, 512)
-        o_im = (p_re[:, 512:] + p_im[:, :512]).reshape(8, 16, 512)
+        o_re = prod[:, :512].reshape(8, 16, 512)
+        o_im = prod[:, 512:].reshape(8, 16, 512)
         part[dz, :, :, 0:16, :] = (o_re * w_re - o_im * w_im).reshape(2, 4, 16, 512)
         part[dz, :, :, 16:32, :] = (o_re * w_im + o_im * w_re).reshape(2, 4, 16, 512)
-        core_copy(dz).start()
+
+    def apart(step, value):
+        def body(index, carry):
+            step(value)
+            return carry
+
+        lax.fori_loop(0, 1 + facet // 16, body, 0)
 
     def multiply(dz, where):
         high, low = xh[:, where], xl[:, where]
         t_high, t_low = th[dz, where, :], tl[dz, where, :]
         return dot(high, t_high) + dot(low, t_high) + dot(high, t_low)
 
+    def prepare(index):
+        where = slice(index * WIDTH, index * WIDTH + WIDTH)
+        cols = index * WIDTH + iota((8, WIDTH), 1)
+        c_re, c_im = turned(sub * 1031 * cols, 65536)
+        c_re, c_im = c_re[0:1], c_im[0:1]
+        s_re, s_im = raw[:, where], raw[:, slice(2048 + where.start, 2048 + where.stop)]
+        for half, moved in enumerate((s_re * c_re - s_im * c_im, s_re * c_im + s_im * c_re)):
+            start = (2 * index + half) * WIDTH
+            high, low = split(moved)
+            xh[:, start : start + WIDTH] = high
+            xl[:, start : start + WIDTH] = low
+
+    cut = cut_taper(window[...])
+    tap[:, 0, :] = cut[:, :128]
+    tap[:, 1, :] = cut[:, 128:]
     picks[...] = jnp.zeros_like(picks)
     for other_z in range(4):
         for other_x in range(4):
             value = pick_ref[other_x * 4 + other_z].astype(F32)
             picks[other_z, other_x : other_x + 1, :] = jnp.full((1, 128), value, F32)
 
-    acc = None
     for index in range(PIECES):
-        raw_copy(index).wait()
-        raw_copy(index + PIECES).wait()
-        where = slice(index * width, index * width + width)
-        cols = index * width + iota((8, width), 1)
-        c_re, c_im = turned(sub * 1031 * cols, 65536)
-        c_re, c_im = c_re[0:1], c_im[0:1]
-        s_re, s_im = raw[:, where], raw[:, slice(2048 + where.start, 2048 + where.stop)]
-        for half, moved in enumerate((s_re * c_re - s_im * c_im, s_re * c_im + s_im * c_re)):
-            high, low = split(moved)
-            xh[half * 256 : half * 256 + 256, where] = high
-            xl[half * 256 : half * 256 + 256, where] = low
-        if index == 0:
-            for copy in t_copies(order[0]):
-                copy.wait()
-        more = multiply(order[0], where)
-        acc = more if acc is None else acc + more
+        for copy in piece_copies(index):
+            copy.wait()
+        if index:
+            for copy in t_copies(order[index]):
+                copy.start()
+        apart(prepare, index)
+        def piece(index):
+            more = multiply(order[0], slice(2 * index * WIDTH, 2 * (index + 1) * WIDTH))
+            acc[...] = more if index == 0 else acc[...] + more
+        apart(piece, index)
+    apart(finish, 2)
     pl.semaphore_wait(barrier, 37)
-    finish(2, acc)
+    core_copy(2).start()
 
     def tap_start(step, carry):
         tap_copy(step).start()
@@ -284,9 +332,11 @@
     def chunk(dz, between):
         for copy in t_copies(dz):
             copy.wait()
-        acc = multiply(dz, slice(0, 1024))
+        acc[...] = multiply(dz, slice(0, 2048))
         between()
-        finish(dz, acc + multiply(dz, slice(1024, 2048)))
+        acc[...] += multiply(dz, slice(2048, 4096))
+        apart(finish, dz)
+        core_copy(dz).start()
 
     chunk(1, lambda: after_core(2))
 
@@ -302,7 +352,9 @@
 
     chunk(0, between_four)
     after_core(0)
+    after_far(0)
     after_y(3)
+    after_far(1)
 
     def tap_wait(step, carry):
         tap_copy(step).wait_send()
@@ -312,9 +364,9 @@
     lax.fori_loop(1, 32, tap_wait, 0)
     taper = placed_taper(tap_out[...])
     after_y(0)
-    for dz in (2, 1, 3):
-        z_copy(dz).wait()
-    sums = (tot[0] + got_z[0]) + (got_z[1] + got_z[2])
+    z_copy(0).wait()
+    z_copy(1).wait()
+    sums = tot[0] + (got_z[0] + got_z[1])
 
     tapered = sums * jnp.concatenate([taper, taper], 0)
     prod = dot3(tapered, ph[...], pw[...])
@@ -335,35 +387,39 @@
             {"facet": source * 4 + y},
         )
 
-    def uy_copy(index):
+    def uy_copy(index, dz):
         dy, dc = near[index]
         to = (y + dy) % 4
-        return remote(
-            zbuf.at[:, to // 2], ybuf.at[c, y], uy_send.at[index], uy_recv.at[index],
-            {"facet": z * 4 + to, "vis": (c + dc) % 2},
-        )
-
-    def uy_arrival(index):
+        source = (z - dz + 4) % 4
+        return remote(
+            zbuf.at[source, to // 2], ybuf.at[c, y, source], uy_send.at[index, dz],
+            uy_recv.at[index, dz], {"facet": z * 4 + to, "vis": (c + dc) % 2},
+        )
+
+    def uy_arrival(index, dz):
         dy, dc = near[index]
-        source = (y - dy + 4) % 4
-        return remote(
-            zbuf.at[:, 0], ybuf.at[(c + dc) % 2, source], uy_send.at[index], uy_recv.at[index],
-            {"facet": z * 4 + source, "vis": (c + dc) % 2},
+        origin = (y - dy + 4) % 4
+        source = (z - dz + 4) % 4
+        return remote(
+            zbuf.at[source, 0], ybuf.at[(c + dc) % 2, origin, source], uy_send.at[index, dz],
+            uy_recv.at[index, dz], {"facet": z * 4 + origin, "vis": (c + dc) % 2},
         )
 
     for dz in (2, 1, 3):
         uz_copy(dz).start()
     zbuf[z] = ubuf[z]
-    for dz in (1, 3, 2):
-        uz_arrival(dz).wait_recv()
-    for index in range(7):
-        uy_copy(index).start()
+    for dz in (0, 1, 3, 2):
+        if dz:
+            uz_arrival(dz).wait_recv()
+        for index in (4, 3, 2, 1, 6, 5, 0):
+            uy_copy(index, dz).start()
     ybuf[c, y] = zbuf[:, y // 2]
     for dz in (1, 2, 3):
         uz_copy(dz).wait_send()
-    for index in range(7):
-        uy_copy(index).wait_send()
-        uy_arrival(index).wait_recv()
+    for dz in (0, 1, 3, 2):
+        for index in range(7):
+            uy_copy(index, dz).wait_send()
+            uy_arrival(index, dz).wait_recv()
     cols = ybuf[...].reshape(512, 128).T
     where = pl.ds(pl.multiple_of(((y % 2) * 2 + c) * 256, 256), 256)
     prod = dot3(cols, ph[:, where], pw[:, where])
@@ -422,7 +478,7 @@
             x_arrival(dx, dz).wait_recv()
 
 
-def shared_patches(strip, tap, pick_row):
+def shared_patches(strip, window, pick_row):
     dma = pltpu.SemaphoreType.DMA
     tables = [jnp.asarray(x) for x in column_table() + row_table()]
     ph, pw = (jnp.asarray(x) for x in grid_table())
@@ -433,16 +489,19 @@
         in_specs=[far] * 3 + [VM] * 5 + [pl.BlockSpec(memory_space=pltpu.SMEM)],
         out_specs=VM,
         scratch_shapes=[
+            pltpu.VMEM((32, 2, 128), F32),
+            pltpu.VMEM((256, 256), F32),
             pltpu.VMEM((256, 4096), F32),
-            pltpu.VMEM((512, 2048), BF16),
-            pltpu.VMEM((512, 2048), BF16),
-            pltpu.VMEM((4, 2048, 256), BF16),
-            pltpu.VMEM((4, 2048, 256), BF16),
+            pltpu.VMEM((256, 4096), BF16),
+            pltpu.VMEM((256, 4096), BF16),
+            pltpu.VMEM((4, 4096, 256), BF16),
+            pltpu.VMEM((4, 4096, 256), BF16),
             pltpu.VMEM((4, 2, 4, 32, 512), F32),
             pltpu.VMEM((4, 4, 32, 512), F32),
             pltpu.VMEM((4, 3, 32, 512), F32),
             pltpu.VMEM((4, 32, 512), F32),
-            pltpu.VMEM((3, 32, 512), F32),
+            pltpu.VMEM((2, 16, 512), F32),
+            pltpu.VMEM((2, 32, 512), F32),
             pltpu.VMEM((32, 2, 128), F32),
             pltpu.VMEM((4, 2, 16, 128), F32),
             pltpu.VMEM((4, 2, 16, 128), F32),
@@ -452,46 +511,50 @@
             pltpu.VMEM((3, 2, 64, 128), F32),
             pltpu.VMEM((3, 8, 128), F32),
             pltpu.VMEM((3, 4, 64, 128), F32),
-            dma((2 * PIECES,)), dma((4, 2)),
-            dma((4,)), dma((4,)), dma((4, 3)), dma((4, 3)), dma((3,)), dma((3,)),
+            dma((PIECES, 4)), dma((4, 2)),
+            dma((4,)), dma((4,)), dma((4, 3)), dma((4, 3)), dma((2,)), dma((2,)), dma((2,)), dma((2,)),
             dma((32,)), dma((32,)),
-            dma((3,)), dma((3,)), dma((7,)), dma((7,)),
+            dma((3,)), dma((3,)), dma((7, 4)), dma((7, 4)),
             dma((3,)), dma((3,)), dma((3,)), dma((3,)), dma((3, 4)), dma((3, 4)),
         ],
         compiler_params=pltpu.CompilerParams(
             collective_id=0, has_side_effects=True, vmem_limit_bytes=58 << 20
         ),
-    )(strip, *tables, tap, ph, pw, pick_row)
+    )(strip, *tables, window, ph, pw, pick_row)
 
 
 def degrid_kernel(owners, patches, tiles, offsets, eh, el, fh, fl, out):
     low_lane = iota((64, 128), 1) < 64
     cells = iota((64, 1024), 0)
-
-    def one(base, carry):
+    mixed = []
+    for base in range(8):
         patch = patches[owners[base]]
         tile = tiles[base]
         straight = patch * tile
         crossed = patch * pltpu.roll(tile, 64, 1)
-        mixed = jnp.where(
-            low_lane, straight - pltpu.roll(straight, 64, 1), crossed + pltpu.roll(crossed, 64, 1)
-        )
-        along = dot3(mixed, eh[...], el[...])
-        quad = dot3(along.T, fh[...], fl[...])
+        mixed.append(
+            jnp.where(
+                low_lane,
+                straight - pltpu.roll(straight, 64, 1),
+                crossed + pltpu.roll(crossed, 64, 1),
+            )
+        )
+    along = dot3(jnp.concatenate(mixed, 0), eh[...], el[...])
+    across = jnp.concatenate([along[64 * base : 64 * base + 64].T for base in range(8)], 0)
+    quads = dot3(across, fh[...], fl[...])
+    for base in range(8):
+        quad = quads[128 * base : 128 * base + 128]
         re = quad[:64, :64] - quad[64:, 64:]
         im = quad[:64, 64:] + quad[64:, :64]
         high, low = split(jnp.concatenate([re, im], 0))
         pair = jnp.concatenate([high, low], 1)
         spot = offsets[base]
-        hot = jnp.where(cells == spot[0:1], 1.0, 0.0).astype(BF16)
+        hot = ones_where(cells == spot[0:1])
         rows = dot(pair, jnp.concatenate([hot, hot], 0))
         hit = cells == spot[1:2]
         vis_re = jnp.sum(jnp.where(hit, rows[:64], 0.0), 0, keepdims=True)
         vis_im = jnp.sum(jnp.where(hit, rows[64:], 0.0), 0, keepdims=True)
         out[base] = jnp.concatenate([vis_re, vis_im], 0)
-        return carry
-
-    lax.fori_loop(0, 8, one, 0, unroll=True)
 
 
 def degrid(owners, patches, tiles, offsets):
@@ -506,8 +569,7 @@
 
 
 def local(facet_strips, taper, send_pick, bl_owner, phase_tiles, cell_offsets):
-    tap = taper[0].T.reshape(32, 2, 128)
-    patches = shared_patches(facet_strips[0], tap, send_pick[0, 0, 0])
+    patches = shared_patches(facet_strips[0], taper[0], send_pick[0, 0, 0])
     result = degrid(bl_owner[0, 0, 0], patches, phase_tiles[0, 0, 0], cell_offsets[0, 0, 0])
     return result[None, None, None]
 

time: 83.6 us -> 77 us (0.921)
  the two profiles are of different devices: /device:TPU:32 before, /device:TPU:64 now
where the time goes in v3:
time: 77 us; the launch traced here: 76.8 us
  Pallas kernels  75.7 us (98%)
  local copies, waits for them, and re-layouts  1.07 us (1%)
    pallas_call x1, Pallas kernels, shared_patches(): pl.pallas_call(patch_kernel, out_shape=jax.ShapeDtypeStruct((16, 64, 128)...  72 us
    pallas_call x1, Pallas kernels, degrid(): pl.pallas_call(degrid_kernel, out_shape=jax.ShapeDtypeStruct((8, 2, 1024)...  3.67 us

profile of v3, /device:TPU:64, one launch (start us, length us, event | category | flops | bytes accessed | tf_op | source)
XLA Modules:
  0.0 76.8 jit_solution(9700362702964936534)
XLA Ops:
  0.0 0.0 copy-start.1
  0.0 0.0 copy-start.2
  0.0 0.0 copy-start.3
  0.0 0.0 copy-start.4
  0.0 0.0 copy-start.5
  0.0 0.0 copy-start.6
  0.0 0.0 copy-start.7
  0.1 72.0 %shard_map.154.patches = f32[16,64,128]{2,1,0:T(8,128)} custom-call(f32[256,4096]{1,0:T(8,128)} %bitcast.10, bf16[4,4096,256]{2,1,0:T(8,128)(2,1)} %constant.20.clone.th_hbm, bf16[4,4096,256]{2,1,0:T(8,128)(2,1)} %constant.21.clone.tl_hbm, bf16[512,1024]{1,0:T(8,128)(2,1)} %constant.22.clone.lh_ref, bf16[512,1024]{1,0:T(8,128)(2,1)} %constant.23.clone.ll_ref, ...), custom_call_target="tpu_custom_call" | custom-call | tf_op jit(solution)/shard_map/pallas_call | solution.py:486
  72.1 0.0 copy-done.1
  72.1 0.0 copy-done.2
  72.1 0.0 copy-done.3
  72.1 0.0 copy-done.4
  72.1 0.0 copy-done.5
  72.1 0.0 copy-done.6
  72.1 0.0 copy-done.7
  72.1 0.0 copy-start
  72.1 1.0 %copy-done = f32[16,64,128]{2,1,0:T(8,128)S(1)} copy-done((f32[16,64,128]{2,1,0:T(8,128)S(1)}, f32[16,64,128]{2,1,0:T(8,128)}, u32[]{:S(2)}) %copy-start) | copy-done | bytes 524312
  73.2 3.7 %shard_map.155 = f32[8,2,1024]{2,1,0:T(2,128)} custom-call(s32[8]{0:T(128)S(1)} %bitcast.9, f32[16,64,128]{2,1,0:T(8,128)S(1)} %copy-done, f32[8,64,128]{2,1,0:T(8,128)S(1)} %bitcast.7, s32[8,2,1024]{2,1,0:T(2,128)S(1)} %bitcast.8, bf16[128,128]{1,0:T(8,128)(2,1)S(1)} %copy-done.4, bf16[128,128]{1,0:T(8,128)(2,1)S(1)} %copy-done.3, ...), custom_call_target="tpu_custom_call" | custom-call | tf_op jit(solution)/shard_map/pallas_call | solution.py:562
Async XLA Ops:
  0.0 72.1 %copy-start.1 = (f32[1,1,1,8,64,128]{5,4,3,2,1,0:T(8,128)S(1)}, f32[1,1,1,8,64,128]{5,4,3,2,1,0:T(8,128)}, u32[]{:S(2)}) copy-start(f32[1,1,1,8,64,128]{5,4,3,2,1,0:T(8,128)} %param.20) | copy-start | bytes 786436
  0.0 72.1 %copy-start.2 = (s32[1,1,1,8,2,1024]{5,4,3,2,1,0:T(2,128)S(1)}, s32[1,1,1,8,2,1024]{5,4,3,2,1,0:T(2,128)}, u32[]{:S(2)}) copy-start(s32[1,1,1,8,2,1024]{5,4,3,2,1,0:T(2,128)} %param.21) | copy-start | bytes 196612
  0.0 72.1 %copy-start.3 = (bf16[128,128]{1,0:T(8,128)(2,1)S(1)}, bf16[128,128]{1,0:T(8,128)(2,1)}, u32[]{:S(2)}) copy-start(bf16[128,128]{1,0:T(8,128)(2,1)} %constant.27.clone.el) | copy-start | bytes 98308
  0.0 72.1 %copy-start.4 = (bf16[128,128]{1,0:T(8,128)(2,1)S(1)}, bf16[128,128]{1,0:T(8,128)(2,1)}, u32[]{:S(2)}) copy-start(bf16[128,128]{1,0:T(8,128)(2,1)} %constant.26.clone.eh) | copy-start | bytes 98308
  0.0 72.1 %copy-start.5 = (bf16[64,128]{1,0:T(8,128)(2,1)S(1)}, bf16[64,128]{1,0:T(8,128)(2,1)}, u32[]{:S(2)}) copy-start(bf16[64,128]{1,0:T(8,128)(2,1)} %constant.29.clone.fl) | copy-start | bytes 49156
  0.0 72.1 %copy-start.6 = (bf16[64,128]{1,0:T(8,128)(2,1)S(1)}, bf16[64,128]{1,0:T(8,128)(2,1)}, u32[]{:S(2)}) copy-start(bf16[64,128]{1,0:T(8,128)(2,1)} %constant.28.clone.fh) | copy-start | bytes 49156
  0.0 72.1 %copy-start.7 = (s32[1,1,1,8]{3,2,1,0:T(1,128)S(1)}, s32[1,1,1,8]{3,2,1,0:T(1,128)}, u32[]{:S(2)}) copy-start(s32[1,1,1,8]{3,2,1,0:T(1,128)} %param.19) | copy-start | bytes 100
  72.1 1.0 %copy-start = (f32[16,64,128]{2,1,0:T(8,128)S(1)}, f32[16,64,128]{2,1,0:T(8,128)}, u32[]{:S(2)}) copy-start(f32[16,64,128]{2,1,0:T(8,128)} %shard_map.154.patches) | copy-start | bytes 1572868

commit v4 on v3

--- a/solution.py
+++ b/solution.py
@@ -32,10 +32,7 @@
     freq = np.arange(512).reshape(2, 4, 4, 16).transpose(2, 0, 1, 3).reshape(4, 1, 128)
     cols = np.arange(2048)[None, :, None]
     angle = (33 * freq * cols % 65536) * (2.0 * np.pi / 65536)
-    cos, sin = np.cos(angle), -np.sin(angle)
-    top = np.concatenate([cos, sin], 2).reshape(4, PIECES, 1, WIDTH, 256)
-    bottom = np.concatenate([-sin, cos], 2).reshape(4, PIECES, 1, WIDTH, 256)
-    return halves(np.concatenate([top, bottom], 2).reshape(4, 4096, 256))
+    return halves(np.concatenate([np.cos(angle), -np.sin(angle)], 2))
 
 
 @functools.lru_cache(None)
@@ -143,11 +140,47 @@
     return jnp.sum(jnp.where(hit, wide, 0.0).reshape(16, 16, 512), 1)
 
 
+def degrid(owners, patches, tiles, offsets, hots, eh, el, fh, fl, out):
+    low_lane = iota((64, 128), 1) < 64
+    cells = iota((64, 1024), 0)
+    mixed = []
+    for base in range(8):
+        patch = patches[owners[base]]
+        tile = tiles[base]
+        straight = patch * tile
+        crossed = patch * pltpu.roll(tile, 64, 1)
+        mixed.append(
+            jnp.where(
+                low_lane,
+                straight - pltpu.roll(straight, 64, 1),
+                crossed + pltpu.roll(crossed, 64, 1),
+            )
+        )
+    along = dot3(jnp.concatenate(mixed, 0), eh[...], el[...])
+    across = jnp.concatenate([along[64 * base : 64 * base + 64].T for base in range(8)], 0)
+    quads = dot3(across, fh[...], fl[...])
+    for base in range(8):
+        quad = quads[128 * base : 128 * base + 128]
+        re = quad[:64, :64] - quad[64:, 64:]
+        im = quad[:64, 64:] + quad[64:, :64]
+        high, low = split(jnp.concatenate([re, im], 0))
+        pair = jnp.concatenate([high, low], 1)
+        spot = offsets[base]
+        hot = hots[base]
+        rows = dot(pair, jnp.concatenate([hot, hot], 0))
+        hit = cells == spot[1:2]
+        vis_re = jnp.sum(jnp.where(hit, rows[:64], 0.0), 0, keepdims=True)
+        vis_im = jnp.sum(jnp.where(hit, rows[64:], 0.0), 0, keepdims=True)
+        out[base] = jnp.concatenate([vis_re, vis_im], 0)
+
+
 def patch_kernel(
-    strip, th_hbm, tl_hbm, lh_ref, ll_ref, window, ph, pw, pick_ref, out,
+    strip, th_hbm, tl_hbm, window, pick_ref, owners,
+    lh_hbm, ll_hbm, ph_hbm, pw_hbm, tiles_hbm, offsets_hbm, eh_hbm, el_hbm, fh_hbm, fl_hbm, vis,
+    lh_ref, ll_ref, ph, pw, tiles, offsets, eh, el, fh, fl, out, hot,
     tap, acc, raw, xh, xl, th, tl, part, got_core, got_y, tot, got_far, got_z, tap_out,
     ubuf, zbuf, ybuf, own, picks, zpatch, zpick, staged,
-    raw_sem, t_sem, core_send, core_recv, y_send, y_recv, far_send, far_recv, z_send, z_recv, tap_send, tap_recv,
+    late_sem, raw_sem, t_sem, core_send, core_recv, y_send, y_recv, far_send, far_recv, z_send, z_recv, tap_send, tap_recv,
     uz_send, uz_recv, uy_send, uy_recv, w_send, w_recv, p_send, p_recv, x_send, x_recv,
 ):
     z, y, x, w, c = here()
@@ -157,7 +190,7 @@
 
     def piece_copies(index):
         re, im = pl.ds(index * WIDTH, WIDTH), pl.ds(2048 + index * WIDTH, WIDTH)
-        rows, at = pl.ds(index * 2 * WIDTH, 2 * WIDTH), (z + order[0]) % 4
+        rows, at = re, (z + order[0]) % 4
         return (
             pltpu.make_async_copy(strip.at[:, re], raw.at[:, re], raw_sem.at[index, 0]),
             pltpu.make_async_copy(strip.at[:, im], raw.at[:, im], raw_sem.at[index, 1]),
@@ -175,6 +208,19 @@
     for index in range(PIECES):
         for copy in piece_copies(index):
             copy.start()
+    late = [
+        pltpu.make_async_copy(source, target, late_sem.at[index])
+        for index, (source, target) in enumerate(
+            (
+                (lh_hbm, lh_ref), (ll_hbm, ll_ref), (ph_hbm, ph), (pw_hbm, pw),
+                (tiles_hbm, tiles), (offsets_hbm, offsets),
+                (eh_hbm, eh), (el_hbm, el), (fh_hbm, fh), (fl_hbm, fl),
+            )
+        )
+    ]
+    for copy in late[:2]:
+        copy.start()
+
     barrier = pltpu.get_barrier_semaphore()
 
     def greet(step, carry):
@@ -265,8 +311,8 @@
     w_re, w_im = (w_re * SCALE)[None], (w_im * SCALE)[None]
 
     def finish(dz):
-        turned_acc = acc[...].T
-        a_re, a_im = turned_acc[:128], turned_acc[128:]
+        a_re = (acc[:256, :128] - acc[256:, 128:]).T
+        a_im = (acc[:256, 128:] + acc[256:, :128]).T
         both = jnp.concatenate([a_re * r_re - a_im * r_im, a_re * r_im + a_im * r_re], 1)
         prod = dot3(both, lh_ref[...], ll_ref[...])
         o_re = prod[:, :512].reshape(8, 16, 512)
@@ -293,10 +339,9 @@
         c_re, c_im = c_re[0:1], c_im[0:1]
         s_re, s_im = raw[:, where], raw[:, slice(2048 + where.start, 2048 + where.stop)]
         for half, moved in enumerate((s_re * c_re - s_im * c_im, s_re * c_im + s_im * c_re)):
-            start = (2 * index + half) * WIDTH
             high, low = split(moved)
-            xh[:, start : start + WIDTH] = high
-            xl[:, start : start + WIDTH] = low
+            xh[half * 256 : half * 256 + 256, where] = high
+            xl[half * 256 : half * 256 + 256, where] = low
 
     cut = cut_taper(window[...])
     tap[:, 0, :] = cut[:, :128]
@@ -315,9 +360,13 @@
                 copy.start()
         apart(prepare, index)
         def piece(index):
-            more = multiply(order[0], slice(2 * index * WIDTH, 2 * (index + 1) * WIDTH))
+            more = multiply(order[0], slice(index * WIDTH, (index + 1) * WIDTH))
             acc[...] = more if index == 0 else acc[...] + more
         apart(piece, index)
+    for copy in late[:2]:
+        copy.wait()
+    for copy in late[2:]:
+        copy.start()
     apart(finish, 2)
     pl.semaphore_wait(barrier, 37)
     core_copy(2).start()
@@ -332,9 +381,9 @@
     def chunk(dz, between):
         for copy in t_copies(dz):
             copy.wait()
-        acc[...] = multiply(dz, slice(0, 2048))
+        acc[...] = multiply(dz, slice(0, 1024))
         between()
-        acc[...] += multiply(dz, slice(2048, 4096))
+        acc[...] += multiply(dz, slice(1024, 2048))
         apart(finish, dz)
         core_copy(dz).start()
 
@@ -367,6 +416,9 @@
     z_copy(0).wait()
     z_copy(1).wait()
     sums = tot[0] + (got_z[0] + got_z[1])
+
+    for copy in late[2:]:
+        copy.wait()
 
     tapered = sums * jnp.concatenate([taper, taper], 0)
     prod = dot3(tapered, ph[...], pw[...])
@@ -450,6 +502,12 @@
             x_recv.at[dx - 1, dz], {"sub": origin * 4 + w},
         )
 
+    cells = iota((64, 1024), 0)
+
+    def mark(unused):
+        for base in range(8):
+            hot[base] = ones_where(cells == offsets[base, 0:1, :])
+
     for dz in (2, 1, 3):
         for copy in w_copies(dz):
             copy.start()
@@ -469,6 +527,8 @@
                 x_copy(dx, dz).start()
             else:
                 out[x * 4 + source] = value
+        if dz == 0:
+            apart(mark, 0)
     for dz in (1, 2, 3):
         for copy in w_copies(dz):
             copy.wait_send()
@@ -476,26 +536,41 @@
         for dx in (1, 3, 2):
             x_copy(dx, dz).wait_send()
             x_arrival(dx, dz).wait_recv()
-
-
-def shared_patches(strip, window, pick_row):
+    degrid(owners, out, tiles, offsets, hot, eh, el, fh, fl, vis)
+
+
+def predicted(strip, window, pick_row, owners, tiles, offsets):
     dma = pltpu.SemaphoreType.DMA
-    tables = [jnp.asarray(x) for x in column_table() + row_table()]
-    ph, pw = (jnp.asarray(x) for x in grid_table())
+    column = [jnp.asarray(x) for x in column_table()]
+    rest = [jnp.asarray(x) for x in row_table() + grid_table()]
+    cells = [jnp.asarray(x) for x in cell_tables()]
     far = pl.BlockSpec(memory_space=pl.ANY)
+    small = pl.BlockSpec(memory_space=pltpu.SMEM)
     return pl.pallas_call(
         patch_kernel,
-        out_shape=jax.ShapeDtypeStruct((16, 64, 128), F32),
-        in_specs=[far] * 3 + [VM] * 5 + [pl.BlockSpec(memory_space=pltpu.SMEM)],
+        out_shape=jax.ShapeDtypeStruct((8, 2, 1024), F32),
+        in_specs=[far] * 3 + [VM, small, small] + [far] * 10,
         out_specs=VM,
         scratch_shapes=[
+            pltpu.VMEM((512, 1024), BF16),
+            pltpu.VMEM((512, 1024), BF16),
+            pltpu.VMEM((512, 1024), BF16),
+            pltpu.VMEM((512, 1024), BF16),
+            pltpu.VMEM((8, 64, 128), F32),
+            pltpu.VMEM((8, 2, 1024), jnp.int32),
+            pltpu.VMEM((128, 128), BF16),
+            pltpu.VMEM((128, 128), BF16),
+            pltpu.VMEM((64, 128), BF16),
+            pltpu.VMEM((64, 128), BF16),
+            pltpu.VMEM((16, 64, 128), F32),
+            pltpu.VMEM((8, 64, 1024), BF16),
             pltpu.VMEM((32, 2, 128), F32),
-            pltpu.VMEM((256, 256), F32),
+            pltpu.VMEM((512, 256), F32),
             pltpu.VMEM((256, 4096), F32),
-            pltpu.VMEM((256, 4096), BF16),
-            pltpu.VMEM((256, 4096), BF16),
-            pltpu.VMEM((4, 4096, 256), BF16),
-            pltpu.VMEM((4, 4096, 256), BF16),
+            pltpu.VMEM((512, 2048), BF16),
+            pltpu.VMEM((512, 2048), BF16),
+            pltpu.VMEM((4, 2048, 256), BF16),
+            pltpu.VMEM((4, 2048, 256), BF16),
             pltpu.VMEM((4, 2, 4, 32, 512), F32),
             pltpu.VMEM((4, 4, 32, 512), F32),
             pltpu.VMEM((4, 3, 32, 512), F32),
@@ -511,7 +586,7 @@
             pltpu.VMEM((3, 2, 64, 128), F32),
             pltpu.VMEM((3, 8, 128), F32),
             pltpu.VMEM((3, 4, 64, 128), F32),
-            dma((PIECES, 4)), dma((4, 2)),
+            dma((10,)), dma((PIECES, 4)), dma((4, 2)),
             dma((4,)), dma((4,)), dma((4, 3)), dma((4, 3)), dma((2,)), dma((2,)), dma((2,)), dma((2,)),
             dma((32,)), dma((32,)),
             dma((3,)), dma((3,)), dma((7, 4)), dma((7, 4)),
@@ -520,57 +595,14 @@
         compiler_params=pltpu.CompilerParams(
             collective_id=0, has_side_effects=True, vmem_limit_bytes=58 << 20
         ),
-    )(strip, *tables, window, ph, pw, pick_row)
-
-
-def degrid_kernel(owners, patches, tiles, offsets, eh, el, fh, fl, out):
-    low_lane = iota((64, 128), 1) < 64
-    cells = iota((64, 1024), 0)
-    mixed = []
-    for base in range(8):
-        patch = patches[owners[base]]
-        tile = tiles[base]
-        straight = patch * tile
-        crossed = patch * pltpu.roll(tile, 64, 1)
-        mixed.append(
-            jnp.where(
-                low_lane,
-                straight - pltpu.roll(straight, 64, 1),
-                crossed + pltpu.roll(crossed, 64, 1),
-            )
-        )
-    along = dot3(jnp.concatenate(mixed, 0), eh[...], el[...])
-    across = jnp.concatenate([along[64 * base : 64 * base + 64].T for base in range(8)], 0)
-    quads = dot3(across, fh[...], fl[...])
-    for base in range(8):
-        quad = quads[128 * base : 128 * base + 128]
-        re = quad[:64, :64] - quad[64:, 64:]
-        im = quad[:64, 64:] + quad[64:, :64]
-        high, low = split(jnp.concatenate([re, im], 0))
-        pair = jnp.concatenate([high, low], 1)
-        spot = offsets[base]
-        hot = ones_where(cells == spot[0:1])
-        rows = dot(pair, jnp.concatenate([hot, hot], 0))
-        hit = cells == spot[1:2]
-        vis_re = jnp.sum(jnp.where(hit, rows[:64], 0.0), 0, keepdims=True)
-        vis_im = jnp.sum(jnp.where(hit, rows[64:], 0.0), 0, keepdims=True)
-        out[base] = jnp.concatenate([vis_re, vis_im], 0)
-
-
-def degrid(owners, patches, tiles, offsets):
-    tables = [jnp.asarray(x) for x in cell_tables()]
-    return pl.pallas_call(
-        degrid_kernel,
-        out_shape=jax.ShapeDtypeStruct((8, 2, 1024), F32),
-        in_specs=[pl.BlockSpec(memory_space=pltpu.SMEM)] + [VM] * 7,
-        out_specs=VM,
-        compiler_params=pltpu.CompilerParams(vmem_limit_bytes=40 << 20),
-    )(owners, patches, tiles, offsets, *tables)
+    )(strip, *column, window, pick_row, owners, *rest, tiles, offsets, *cells)
 
 
 def local(facet_strips, taper, send_pick, bl_owner, phase_tiles, cell_offsets):
-    patches = shared_patches(facet_strips[0], taper[0], send_pick[0, 0, 0])
-    result = degrid(bl_owner[0, 0, 0], patches, phase_tiles[0, 0, 0], cell_offsets[0, 0, 0])
+    result = predicted(
+        facet_strips[0], taper[0], send_pick[0, 0, 0], bl_owner[0, 0, 0],
+        phase_tiles[0, 0, 0], cell_offsets[0, 0, 0],
+    )
     return result[None, None, None]
 
 

time: 77 us -> 74.2 us (0.964)
  the two profiles are of different devices: /device:TPU:64 before, /device:TPU:32 now
where the time goes in v4:
time: 74.2 us; the launch traced here: 74 us
  Pallas kernels  72.5 us (98%)
  local copies, waits for them, and re-layouts  1.47 us (2%)
    pallas_call x1, Pallas kernels, predicted(): pl.pallas_call(patch_kernel, out_shape=jax.ShapeDtypeStruct((8, 2, 1024),...  72.5 us

profile of v4, /device:TPU:32, one launch (start us, length us, event | category | flops | bytes accessed | tf_op | source)
XLA Modules:
  0.0 74.0 jit_solution(14169108073006723073)
XLA Ops:
  0.0 72.5 %shard_map.154 = f32[8,2,1024]{2,1,0:T(2,128)} custom-call(f32[256,4096]{1,0:T(8,128)} %bitcast.7, bf16[4,2048,256]{2,1,0:T(8,128)(2,1)} %constant.20.clone.th_hbm, bf16[4,2048,256]{2,1,0:T(8,128)(2,1)} %constant.21.clone.tl_hbm, f32[16,512]{1,0:T(8,128)} %bitcast.11, s32[16]{0:T(128)} %bitcast.12, s32[8]{0:T(128)} %bitcast.13, ...), custom_call_target="tpu_custom_call" | custom-call | tf_op jit(solution)/shard_map/pallas_call | solution.py:549
  72.5 1.5 %copy.18 = f32[1,1,1,8,2,1024]{5,4,3,2,1,0:T(2,128)} copy(f32[1,1,1,8,2,1024]{5,4,3,2,1,0:T(2,128)} %bitcast.9) | data formatting | bytes 131072

commit v5 on v4

--- a/solution.py
+++ b/solution.py
@@ -375,8 +375,6 @@
         tap_copy(step).start()
         return carry
 
-    lax.fori_loop(1, 32, tap_start, 0)
-    tap_out[me] = tap[c * 16 + y * 4 + z]
 
     def chunk(dz, between):
         for copy in t_copies(dz):
@@ -400,6 +398,8 @@
         after_y(1)
 
     chunk(0, between_four)
+    lax.fori_loop(1, 32, tap_start, 0)
+    tap_out[me] = tap[c * 16 + y * 4 + z]
     after_core(0)
     after_far(0)
     after_y(3)

time: 74.2 us -> 74.6 us (level)
  the two profiles are of different devices: /device:TPU:32 before, /device:TPU:8 now
where the time goes in v5:
time: 74.6 us; the launch traced here: 74.4 us
  Pallas kernels  72.9 us (98%)
  local copies, waits for them, and re-layouts  1.47 us (2%)
    pallas_call x1, Pallas kernels, predicted(): pl.pallas_call(patch_kernel, out_shape=jax.ShapeDtypeStruct((8, 2, 1024),...  72.9 us

profile of v5, /device:TPU:8, one launch (start us, length us, event | category | flops | bytes accessed | tf_op | source)
XLA Modules:
  0.0 74.4 jit_solution(5487614340641213342)
XLA Ops:
  0.0 72.9 %shard_map.154 = f32[8,2,1024]{2,1,0:T(2,128)} custom-call(f32[256,4096]{1,0:T(8,128)} %bitcast.7, bf16[4,2048,256]{2,1,0:T(8,128)(2,1)} %constant.20.clone.th_hbm, bf16[4,2048,256]{2,1,0:T(8,128)(2,1)} %constant.21.clone.tl_hbm, f32[16,512]{1,0:T(8,128)} %bitcast.11, s32[16]{0:T(128)} %bitcast.12, s32[8]{0:T(128)} %bitcast.13, ...), custom_call_target="tpu_custom_call" | custom-call | tf_op jit(solution)/shard_map/pallas_call | solution.py:549
  72.9 1.5 %copy.18 = f32[1,1,1,8,2,1024]{5,4,3,2,1,0:T(2,128)} copy(f32[1,1,1,8,2,1024]{5,4,3,2,1,0:T(2,128)} %bitcast.9) | data formatting | bytes 131072
